TPU v7x, 512 devices: a whole 4x4x16 slice. The times are simulated.
512 devices in a mesh: seq: 512 (over x, z, y, core).
Axes of the slice: x: 4, y: 4, z: 16, core: 2. Of those that a mesh axis runs over, the one named last changes fastest.
Arguments:
- hidden: bfloat16 [65536, 2048], P('seq'), may hold values from -24 to 24
- queries: bfloat16 [65536, 2048], P('seq'), may hold values from -6 to 6
- key_rows: bfloat16 [65536, 512], P('seq'), may hold values from -6 to 6
- grad_out: bfloat16 [65536, 2048], P('seq'), may hold values from -6 to 6
- master_value: float32 [2048, 512], P('seq'), may hold values from -0.125 to 0.125
- adam_first: float32 [2048, 512], P('seq'), may hold values from -12 to 12
- adam_second: float32 [2048, 512], P('seq'), may hold values from 1 to 100
Outputs:
- attention: bfloat16 [65536, 2048], P('seq')
- grad_queries: bfloat16 [65536, 2048], P('seq')
- grad_keys: bfloat16 [65536, 512], P('seq')
- grad_hidden: bfloat16 [65536, 2048], P('seq')
- new_master: float32 [2048, 512], P('seq')
- new_first: float32 [2048, 512], P('seq')
- new_second: float32 [2048, 512], P('seq')
All inputs are finite; a program needn't handle non-finite values.
Results may differ from a plain program's by a relative error of at most 0.02.
Values may be sent and summed in bfloat16 or wider, within the bound.
A program may use at most 64 MiB of HBM per device.

v0:
```python
import math

import jax
import jax.numpy as jnp
from jax import lax
from jax.sharding import PartitionSpec as P

HQ = 16
HK = 4
DH = 128
WINDOW = 512
OPT_STEP = 10


beta_first = 0.9
beta_second = 0.95
learning = 0.001
decay_rate = 0.1
epsilon = 1e-08


def passed_along(block, axis, distance):
    devices = range(lax.axis_size(axis))
    route = [(i - distance, i) for i in devices if i - distance in devices]
    return lax.ppermute(block, axis, route)


def attend_block(query_blk, grad_blk, key_win, value_win, allowed):
    ratio = HQ // HK
    scale = 1.0 / math.sqrt(DH)
    count = query_blk.shape[0]
    out_parts, dq_parts, dk_parts, dv_parts = ([], [], [], [])
    for group in range(HK):
        low = group * ratio * DH
        high = (group + 1) * ratio * DH
        query_group = query_blk[:, low:high].reshape(count, ratio, DH)
        grad_group = grad_blk[:, low:high].reshape(count, ratio, DH)
        key_group = key_win[:, group * DH : (group + 1) * DH]
        value_group = value_win[:, group * DH : (group + 1) * DH]
        scores = (
            jnp.einsum("trd,sd->trs", query_group, key_group, preferred_element_type=jnp.float32)
            * scale
        )
        scores = jnp.where(allowed[:, None, :], scores, -jnp.inf)
        top = jnp.max(scores, axis=2, keepdims=True)
        expd = jnp.exp(scores - top)
        probs = expd / jnp.sum(expd, axis=2, keepdims=True)
        probs_low = probs.astype(jnp.bfloat16)
        out_group = jnp.einsum(
            "trs,sd->trd", probs_low, value_group, preferred_element_type=jnp.float32
        ).astype(jnp.bfloat16)
        delta = jnp.sum(
            grad_group.astype(jnp.float32) * out_group.astype(jnp.float32), axis=2, keepdims=True
        )
        dprob = jnp.einsum(
            "trd,sd->trs", grad_group, value_group, preferred_element_type=jnp.float32
        )
        dscore = (probs * (dprob - delta)).astype(jnp.bfloat16)
        dq_group = (
            jnp.einsum("trs,sd->trd", dscore, key_group, preferred_element_type=jnp.float32) * scale
        ).astype(jnp.bfloat16)
        dk_group = (
            jnp.einsum("trs,trd->sd", dscore, query_group, preferred_element_type=jnp.float32)
            * scale
        )
        dv_group = jnp.einsum(
            "trs,trd->sd", probs_low, grad_group, preferred_element_type=jnp.float32
        )
        out_parts.append(out_group.reshape(count, ratio * DH))
        dq_parts.append(dq_group.reshape(count, ratio * DH))
        dk_parts.append(dk_group)
        dv_parts.append(dv_group)
    return (
        jnp.concatenate(out_parts, 1),
        jnp.concatenate(dq_parts, 1),
        jnp.concatenate(dk_parts, 1),
        jnp.concatenate(dv_parts, 1),
    )


def shards(hidden, queries, key_rows, grad_out, master_value, adam_first, adam_second):
    tok_rows = hidden.shape[0]
    reach = WINDOW // tok_rows
    position = lax.axis_index("seq")
    weight_low = master_value.astype(jnp.bfloat16)
    weight_full = lax.all_gather(weight_low, "seq", axis=0, tiled=True)
    values = jnp.dot(hidden, weight_full, preferred_element_type=jnp.float32).astype(jnp.bfloat16)
    earlier = []
    for distance in range(1, reach + 1):
        earlier.append(passed_along((key_rows, values), "seq", distance))
    ordered = earlier[::-1]
    key_win = jnp.concatenate([entry[0] for entry in ordered] + [key_rows], 0)
    value_win = jnp.concatenate([entry[1] for entry in ordered] + [values], 0)
    span_rows = (reach + 1) * tok_rows
    key_index = jnp.arange(span_rows, dtype=jnp.int32)
    key_pos = position * tok_rows - WINDOW + key_index
    relative = jnp.arange(tok_rows, dtype=jnp.int32)[:, None] + WINDOW - key_index[None, :]
    allowed = (relative >= 0) & (relative < WINDOW) & (key_pos >= 0)[None, :]
    attention, grad_queries, dk_win, dv_win = attend_block(
        queries, grad_out, key_win, value_win, allowed
    )

    def partial_terms(distance):
        low = (reach - distance) * tok_rows
        return (dk_win[low : low + tok_rows], dv_win[low : low + tok_rows])

    key_total, value_total = partial_terms(0)
    for distance in range(1, reach + 1):
        arrived = passed_along(partial_terms(distance), "seq", -distance)
        key_total = key_total + arrived[0]
        value_total = value_total + arrived[1]
    grad_keys = key_total.astype(jnp.bfloat16)
    d_value = value_total.astype(jnp.bfloat16)
    grad_hidden = lax.dot_general(
        d_value, weight_full, (((1,), (1,)), ((), ())), preferred_element_type=jnp.float32
    ).astype(jnp.bfloat16)
    grad_weight = lax.psum_scatter(
        lax.dot_general(
            hidden, d_value, (((0,), (0,)), ((), ())), preferred_element_type=jnp.float32
        ),
        "seq",
        scatter_dimension=0,
        tiled=True,
    )
    new_first = beta_first * adam_first + (1.0 - beta_first) * grad_weight
    new_second = beta_second * adam_second + (1.0 - beta_second) * grad_weight * grad_weight
    first_hat = new_first / (1.0 - beta_first**OPT_STEP)
    second_hat = new_second / (1.0 - beta_second**OPT_STEP)
    new_master = master_value - learning * (
        first_hat / (jnp.sqrt(second_hat) + epsilon) + decay_rate * master_value
    )
    return (attention, grad_queries, grad_keys, grad_hidden, new_master, new_first, new_second)


def solution(mesh):
    placed = (
        P("seq", None),
        P("seq", None),
        P("seq", None),
        P("seq", None),
        P("seq", None),
        P("seq", None),
        P("seq", None),
    )
    return jax.shard_map(
        shards,
        mesh=mesh,
        in_specs=placed,
        out_specs=(
            P("seq", None),
            P("seq", None),
            P("seq", None),
            P("seq", None),
            P("seq", None),
            P("seq", None),
            P("seq", None),
        ),
        check_vma=False,
    )
```

profile of v0, /device:TPU:1, one launch (start us, length us, event | category | flops | bytes accessed | tf_op | source)
XLA Modules:
  0.0 829.3 jit_solution(7328140759621457973)
XLA Ops:
  7.2 5.8 collective-permute-start
  13.0 4.2 collective-permute-start.1
  17.2 3.2 collective-permute-start.2
  20.4 1.9 collective-permute-start.3
  28.2 2.5 fusion.77
  30.7 2.5 fusion.76
  33.2 2.5 fusion.75
  37.2 1.9 fusion.40
  43.1 2.4 collective-permute-start.12
  49.4 2.3 collective-permute-done.12
  51.7 4.1 collective-permute-done.13
  55.8 2.5 collective-permute-done.14
  58.2 3.1 collective-permute-done.15
  61.4 2.7 convolution_bitcast_fusion
  64.2 503.0 %all-reduce.3.cloned.1.call-done = f32[2048,512]{0,1:T(8,128)} async-done(((f32[2048,512]{0,1:T(8,128)}), f32[2048,512]{0,1:T(8,128)}) %all-reduce.3.cloned.1.call-update) | async-done | bytes 4194320
  569.1 197.4 %all-gather.3.cloned.1.call-done = bf16[512,4,512]{2,1,0:T(4,128)(2,1)} async-done(((bf16[1,4,512]{2,1,0:T(4,128)(2,1)}), bf16[512,4,512]{2,1,0:T(4,128)(2,1)}) %all-gather.3.cloned.1.call-update) | async-done | bytes 2097168 | tf_op jit(solution)/shard_map/all_gather | solution.py:86
  766.5 2.5 reshape.133
  769.5 4.6 collective-permute-start.4
  774.2 3.2 collective-permute-start.5
  779.0 3.2 collective-permute-start.6
  782.3 2.4 collective-permute-start.7
  807.7 2.9 collective-permute-done.10
  810.6 2.9 collective-permute-done.11
  813.6 6.6 collective-permute-done.8
  (158 shorter events, 44.0 us)
Async XLA Ops:
  7.2 54.3 %copy-start = (bf16[128,2048]{1,0:T(8,128)(2,1)S(1)}, bf16[128,2048]{1,0:T(8,128)(2,1)}, u32[]{:S(2)}) copy-start(bf16[128,2048]{1,0:T(8,128)(2,1)} %param.7) | copy-start | bytes 1572868
  7.2 560.1 %all-reduce.3.cloned.1.call-start = ((), (), s32[]{:S(2)}) async-start(), calls=%async_computation.1 | async-start | bytes 8388608
  7.2 17.6 %collective-permute-start = (bf16[128,512]{1,0:T(8,128)(2,1)}, bf16[128,512]{1,0:T(8,128)(2,1)S(1)}, u32[]{:S(2)}, u32[]{:S(2)}) collective-permute-start(bf16[128,512]{1,0:T(8,128)(2,1)} %param.9), channel_id=1, source_target_pairs={{0,4},{1,5},{2,6},{3,7},{4,8},{5,9},{6,10},{7,11},{8,12},{9,13},{1... | collective-permute-start | bytes 393224 | tf_op jit(solution)/shard_map/ppermute | solution.py:25
  13.0 12.5 %collective-permute-start.1 = (bf16[128,512]{1,0:T(8,128)(2,1)}, bf16[128,512]{1,0:T(8,128)(2,1)S(1)}, u32[]{:S(2)}, u32[]{:S(2)}) collective-permute-start(bf16[128,512]{1,0:T(8,128)(2,1)} %param.9), channel_id=1, source_target_pairs={{0,3},{1,4},{2,5},{3,6},{4,7},{5,8},{6,9},{7,10},{8,11},{9,12},{10... | collective-permute-start | bytes 393224 | tf_op jit(solution)/shard_map/ppermute | solution.py:25
  17.2 9.0 %collective-permute-start.2 = (bf16[128,512]{1,0:T(8,128)(2,1)}, bf16[128,512]{1,0:T(8,128)(2,1)S(1)}, u32[]{:S(2)}, u32[]{:S(2)}) collective-permute-start(bf16[128,512]{1,0:T(8,128)(2,1)} %param.9), channel_id=1, source_target_pairs={{0,2},{1,3},{2,4},{3,5},{4,6},{5,7},{6,8},{7,9},{8,10},{9,11},{10,... | collective-permute-start | bytes 393224 | tf_op jit(solution)/shard_map/ppermute | solution.py:25
  20.4 6.4 collective-permute-start.3
  24.6 17.2 %copy-start.20 = (bf16[128,512]{0,1:T(8,128)(2,1)}, bf16[128,512]{0,1:T(8,128)(2,1)S(1)}, u32[]{:S(2)}) copy-start(bf16[128,512]{0,1:T(8,128)(2,1)S(1)} %copy.224) | copy-start | bytes 393220
  24.8 17.7 %copy-start.16 = (bf16[128,512]{0,1:T(8,128)(2,1)}, bf16[128,512]{0,1:T(8,128)(2,1)S(1)}, u32[]{:S(2)}) copy-start(bf16[128,512]{0,1:T(8,128)(2,1)S(1)} %copy.228) | copy-start | bytes 393220
  43.1 8.6 %collective-permute-start.12 = (f32[128,512]{0,1:T(8,128)S(1)}, f32[128,512]{0,1:T(8,128)S(1)}, u32[]{:S(2)}, u32[]{:S(2)}) collective-permute-start(f32[128,512]{0,1:T(8,128)S(1)} %get-tuple-element.38), channel_id=1, source_target_pairs={{1,0},{2,1},{3,2},{4,3},{5,4},{6,5},{7,6},{8,7},{9,8},{10,9},{11,1... | collective-permute-start | bytes 786440 | tf_op jit(solution)/shard_map/ppermute | solution.py:25
  45.5 10.3 %collective-permute-start.13 = (f32[128,512]{0,1:T(8,128)S(1)}, f32[128,512]{0,1:T(8,128)S(1)}, u32[]{:S(2)}, u32[]{:S(2)}) collective-permute-start(f32[128,512]{0,1:T(8,128)S(1)} %get-tuple-element.41), channel_id=1, source_target_pairs={{2,0},{3,1},{4,2},{5,3},{6,4},{7,5},{8,6},{9,7},{10,8},{11,9},{12,... | collective-permute-start | bytes 786440 | tf_op jit(solution)/shard_map/ppermute | solution.py:25
  46.8 11.4 %collective-permute-start.14 = (f32[128,512]{0,1:T(8,128)S(1)}, f32[128,512]{0,1:T(8,128)S(1)}, u32[]{:S(2)}, u32[]{:S(2)}) collective-permute-start(f32[128,512]{0,1:T(8,128)S(1)} %get-tuple-element.40), channel_id=1, source_target_pairs={{3,0},{4,1},{5,2},{6,3},{7,4},{8,5},{9,6},{10,7},{11,8},{12,9},{13... | collective-permute-start | bytes 786440 | tf_op jit(solution)/shard_map/ppermute | solution.py:25
  48.1 13.2 %collective-permute-start.15 = (f32[128,512]{0,1:T(8,128)S(1)}, f32[128,512]{0,1:T(8,128)S(1)}, u32[]{:S(2)}, u32[]{:S(2)}) collective-permute-start(f32[128,512]{0,1:T(8,128)S(1)} %get-tuple-element.39), channel_id=1, source_target_pairs={{4,0},{5,1},{6,2},{7,3},{8,4},{9,5},{10,6},{11,7},{12,8},{13,9},{1... | collective-permute-start | bytes 786440 | tf_op jit(solution)/shard_map/ppermute | solution.py:25
  64.1 504.3 %copy-start.32 = (f32[4,512]{1,0:T(4,128)S(1)}, f32[4,512]{1,0:T(4,128)}, u32[]{:S(2)}) copy-start(f32[4,512]{1,0:T(4,128)} %param.11) | copy-start | bytes 24580
  64.1 504.3 %copy-start.33 = (f32[4,512]{1,0:T(4,128)S(1)}, f32[4,512]{1,0:T(4,128)}, u32[]{:S(2)}) copy-start(f32[4,512]{1,0:T(4,128)} %param.12) | copy-start | bytes 24580
  64.1 504.3 %copy-start.34 = (f32[4,512]{1,0:T(4,128)S(1)}, f32[4,512]{1,0:T(4,128)}, u32[]{:S(2)}) copy-start(f32[4,512]{1,0:T(4,128)} %param.13) | copy-start | bytes 24580
  64.2 702.4 %all-gather.3.cloned.1.call-start = ((), (), s32[]{:S(2)}) async-start(), calls=%async_computation | async-start | bytes 2101248 | tf_op jit(solution)/shard_map/all_gather | solution.py:86
  769.5 15.1 %collective-permute-start.4 = (bf16[128,512]{1,0:T(8,128)(2,1)S(1)}, bf16[128,512]{1,0:T(8,128)(2,1)S(1)}, u32[]{:S(2)}, u32[]{:S(2)}) collective-permute-start(bf16[128,512]{1,0:T(8,128)(2,1)S(1)} %convolution_convert_fusion.5), channel_id=1, source_target_pairs={{0,4},{1,5},{2,6},{3,7},{4,8},{5,9},{6,10},{7,11},{8,12},{9,13},{1... | collective-permute-start | bytes 393224 | tf_op jit(solution)/shard_map/ppermute | solution.py:25
  774.2 10.5 %collective-permute-start.5 = (bf16[128,512]{1,0:T(8,128)(2,1)S(1)}, bf16[128,512]{1,0:T(8,128)(2,1)S(1)}, u32[]{:S(2)}, u32[]{:S(2)}) collective-permute-start(bf16[128,512]{1,0:T(8,128)(2,1)S(1)} %convolution_convert_fusion.5), channel_id=1, source_target_pairs={{0,3},{1,4},{2,5},{3,6},{4,7},{5,8},{6,9},{7,10},{8,11},{9,12},{10... | collective-permute-start | bytes 393224 | tf_op jit(solution)/shard_map/ppermute | solution.py:25
  779.0 5.7 collective-permute-start.6
  782.3 4.3 collective-permute-start.7
  798.4 12.2 %collective-permute-start.10 = (f32[128,512]{0,1:T(8,128)}, f32[128,512]{0,1:T(8,128)S(1)}, u32[]{:S(2)}, u32[]{:S(2)}) collective-permute-start(f32[128,512]{0,1:T(8,128)} %get-tuple-element.44), channel_id=1, source_target_pairs={{3,0},{4,1},{5,2},{6,3},{7,4},{8,5},{9,6},{10,7},{11,8},{12,9},{13... | collective-permute-start | bytes 786440 | tf_op jit(solution)/shard_map/ppermute | solution.py:25
  799.7 13.9 %collective-permute-start.11 = (f32[128,512]{0,1:T(8,128)}, f32[128,512]{0,1:T(8,128)S(1)}, u32[]{:S(2)}, u32[]{:S(2)}) collective-permute-start(f32[128,512]{0,1:T(8,128)} %get-tuple-element.43), channel_id=1, source_target_pairs={{4,0},{5,1},{6,2},{7,3},{8,4},{9,5},{10,6},{11,7},{12,8},{13,9},{1... | collective-permute-start | bytes 786440 | tf_op jit(solution)/shard_map/ppermute | solution.py:25
  801.0 19.1 %collective-permute-start.8 = (f32[128,512]{0,1:T(8,128)}, f32[128,512]{0,1:T(8,128)}, u32[]{:S(2)}, u32[]{:S(2)}) collective-permute-start(f32[128,512]{0,1:T(8,128)} %get-tuple-element.42), channel_id=1, source_target_pairs={{1,0},{2,1},{3,2},{4,3},{5,4},{6,5},{7,6},{8,7},{9,8},{10,9},{11,1... | collective-permute-start | bytes 786440 | tf_op jit(solution)/shard_map/ppermute | solution.py:25
  802.9 17.7 %collective-permute-start.9 = (f32[128,512]{0,1:T(8,128)}, f32[128,512]{0,1:T(8,128)}, u32[]{:S(2)}, u32[]{:S(2)}) collective-permute-start(f32[128,512]{0,1:T(8,128)} %get-tuple-element.45), channel_id=1, source_target_pairs={{2,0},{3,1},{4,2},{5,3},{6,4},{7,5},{8,6},{9,7},{10,8},{11,9},{12,... | collective-permute-start | bytes 786440 | tf_op jit(solution)/shard_map/ppermute | solution.py:25
  (29 other events, 140.1 us)
Sparse Core Ops, SparseCore 0:
  64.3 502.9 all-reduce.2
  572.4 194.0 all-gather.2
where the time goes:
time: 835 us; the launch traced here: 829 us
  waiting for transfers between devices  727 us (87%)
  starting transfers between devices  40.8 us (5%)
  matrix products  24.9 us (3%)
  local copies, waits for them, and re-layouts  16 us (2%)
  between operations  14.9 us (2%)
    unnamed x3, waiting for transfers between devices  503 us
    all_gather x1, waiting for transfers between devices, shards(): weight_full = lax.all_gather(weight_low, 'seq', axis=0, tiled=True)  197 us
    ppermute x16, starting transfers between devices, passed_along(): return lax.ppermute(block, axis, route)  40.7 us
    ppermute x16, waiting for transfers between devices, passed_along(): return lax.ppermute(block, axis, route)  26.7 us
  transfers between devices with their start and end apart: 18, of which 11 were waited for; matrix products, arithmetic and copies ran while one was open for 1% of the time, Pallas kernels for 0%

commit v1 on v0

v1 whole, which is shorter than its diff:
```python
import math

import jax
import jax.numpy as jnp
from jax import lax
from jax.experimental import pallas as pl
from jax.experimental.pallas import tpu as pltpu
from jax.sharding import PartitionSpec as P

HQ = 16
HK = 4
DH = 128
WINDOW = 512
OPT_STEP = 10
TOK = 128
SCALE = 1.0 / math.sqrt(DH)

beta_first = 0.9
beta_second = 0.95
learning = 0.001
decay_rate = 0.1
epsilon = 1e-08

F32 = jnp.float32
BF16 = jnp.bfloat16
MESH = pl.DeviceIdType.MESH

NX, NZ, NY = 4, 16, 4
ZL = 8
HALF = 256
QHALF = 1024


def nt(a, b):
    return lax.dot_general(a, b, (((1,), (1,)), ((), ())), preferred_element_type=F32)


def nn(a, b):
    return lax.dot_general(a, b, (((1,), (0,)), ((), ())), preferred_element_type=F32)


def tn(a, b):
    return lax.dot_general(a, b, (((0,), (0,)), ((), ())), preferred_element_type=F32)


def aligned(value, multiple):
    return pl.multiple_of(value, multiple)


def kernel(
    hid_ref, q_ref, k_ref, go_ref, w_ref, m_ref, v_ref,
    o_out, dq_out, gk_out, gh_out, nw_out, nm_out, nv_out,
    hbuf, qbuf, gobuf, kw, vw, wsib, wz, w2, bias, perm, hp, ht, pbuf, dsbuf,
    dvw, dkw, dvs, dvr, dks, dkr, dksib, dksib_s, dval, dx,
    gbuf, r1a, r1b, s1a, s1b, r2, t2, z3, r3, gx, obuf, dqbuf,
    loc, sib_s, sib_r, k_s, k_r, v_s, v_r, dv_s, dv_r, dk_s, dk_r,
    ag1_s, ag1_r, ag2_s, ag2_r, ag3_s, ag3_r, rs1_s, rs1_r, rs2_s, rs2_r, rs3_s, rs3_r,
):
    ZH = NZ // ZL
    ROWS = ZL * 8
    PG = NY * ROWS
    NG = NX * ZH
    NCHIP = NX * NZ * NY
    d = lax.axis_index("seq")
    c = d % 2
    o = 1 - c
    n = d // 2
    y = n % NY
    z = (n // NY) % NZ
    x = n // (NY * NZ)

    def chip(step):
        return (n + step + NCHIP) % NCHIP

    def dev(x_, z_, y_):
        return ((x_ * NZ + z_) * NY + y_) * 2 + c

    sibling = n * 2 + o

    def remote(src, dst, ssem, rsem, device):
        return pltpu.make_async_remote_copy(
            src_ref=src, dst_ref=dst, send_sem=ssem, recv_sem=rsem,
            device_id=(device,), device_id_type=MESH,
        )

    def x_peer(k):
        return (x + k) % NX

    def y_peer(k):
        return (y + k) % NY

    barrier = pltpu.get_barrier_semaphore()

    def greet(device):
        pl.semaphore_signal(barrier, inc=1, device_id=(device,), device_id_type=MESH)

    greet(sibling)
    for step in (-2, -1, 1, 2):
        for h in range(2):
            greet(chip(step) * 2 + h)
    for k in range(1, NX):
        greet(dev(x_peer(k), z, y))
    for k in range(1, NY):
        greet(dev(x, z, y_peer(k)))

    @pl.loop(1, NZ)
    def _(k):
        greet(dev(x, (z + k) % NZ, y))

    pl.semaphore_wait(barrier, 1 + 8 + (NX - 1) + (NY - 1) + (NZ - 1))

    own_q = pl.ds(aligned(c * QHALF, QHALF), QHALF)
    oth_q = pl.ds(aligned(o * QHALF, QHALF), QHALF)
    own_k = pl.ds(aligned(c * HALF, HALF), HALF)
    oth_k = pl.ds(aligned(o * HALF, HALF), HALF)

    send_w = remote(w_ref.at[:, oth_k], wsib.at[c], sib_s.at[0], sib_r.at[0], sibling)
    send_w.start()
    k_sends = [remote(k_ref.at[:, oth_k], kw.at[4 + c], k_s.at[0], k_r.at[4 + c], sibling)]
    for step in (2, 1):
        for h in range(2):
            k_sends.append(
                remote(
                    k_ref.at[:, h * HALF : (h + 1) * HALF],
                    kw.at[(2 - step) * 2 + c],
                    k_s.at[len(k_sends)],
                    k_r.at[(2 - step) * 2 + c],
                    chip(step) * 2 + h,
                )
            )
    for copy in k_sends:
        copy.start()
    local = [
        pltpu.make_async_copy(k_ref.at[:, own_k], kw.at[4 + c], loc.at[0]),
        pltpu.make_async_copy(q_ref.at[:, own_q], qbuf.at[c], loc.at[1]),
        pltpu.make_async_copy(go_ref.at[:, own_q], gobuf.at[c], loc.at[2]),
        pltpu.make_async_copy(hid_ref, hbuf.at[c], loc.at[3]),
    ]
    for copy in local:
        copy.start()
    send_hid = remote(hid_ref, hbuf.at[c], sib_s.at[3], sib_r.at[3], sibling)
    send_q = remote(q_ref.at[:, oth_q], qbuf.at[c], sib_s.at[1], sib_r.at[1], sibling)
    send_go = remote(go_ref.at[:, oth_q], gobuf.at[c], sib_s.at[2], sib_r.at[2], sibling)
    for copy in (send_hid, send_q, send_go):
        copy.start()

    def arrived(dst, ssem, rsem):
        remote(dst, dst, ssem, rsem, sibling).wait_recv()

    wsib[c] = w_ref[:, own_k]
    arrived(wsib.at[o], sib_s.at[0], sib_r.at[0])
    block = jnp.concatenate([wsib[0], wsib[1]], 0)
    wz[z] = jnp.concatenate([block[:, :128], block[:, 128:]], 0).astype(BF16)

    def ag1(k):
        return remote(wz.at[z], wz.at[z], ag1_s.at[k], ag1_r.at[k], dev(x, (z + k) % NZ, y))

    @pl.loop(1, NZ)
    def _(k):
        ag1(k).start()

    row = lax.broadcasted_iota(jnp.int32, (TOK, 5 * TOK), 0)
    col = lax.broadcasted_iota(jnp.int32, (TOK, 5 * TOK), 1)
    relative = row + WINDOW - col
    for t in range(2):
        first = (d - c + t) * TOK - WINDOW
        allowed = (relative >= 0) & (relative < WINDOW) & (col + first >= 0)
        bias[t] = jnp.where(allowed, 0.0, -1e30).astype(F32)
    prow = lax.broadcasted_iota(jnp.int32, (PG, PG), 0)
    pcol = lax.broadcasted_iota(jnp.int32, (PG, PG), 1)
    source = ((prow % ROWS) // 8) * (NY * 8) + (prow // ROWS) * 8 + prow % 8
    perm[...] = jnp.where(source == pcol, 1.0, 0.0).astype(BF16)
    dvw[...] = jnp.zeros(dvw.shape, F32)
    dkw[...] = jnp.zeros(dkw.shape, F32)

    local[3].wait()
    arrived(hbuf.at[o], sib_s.at[3], sib_r.at[3])

    @pl.loop(0, NG)
    def _(g):
        cols = pl.ds(aligned(g * PG, PG), PG)
        both = jnp.concatenate([hbuf[0, :, cols], hbuf[1, :, cols]], 0)
        hp[g] = nt(both, perm[...]).astype(BF16)
        ht[g] = nt(perm[...], both).astype(BF16)

    @pl.loop(1, NZ)
    def _(k):
        slot = (z - k + NZ) % NZ
        remote(wz.at[slot], wz.at[slot], ag1_s.at[k], ag1_r.at[k], sibling).wait_recv()

    mine = pl.ds(x * ZH, ZH)
    for zh in range(ZH):
        rows = []
        for zl in range(ZL):
            block = wz[zh * ZL + zl].astype(F32)
            rows.append(jnp.concatenate([block[:8], block[8:]], 1))
        w2[c, x * ZH + zh, y] = jnp.concatenate(rows, 0).astype(BF16)

    def ag2_x(k, who):
        at = w2.at[c, pl.ds(who * ZH, ZH), y]
        return remote(at, at, ag2_s.at[k - 1], ag2_r.at[k - 1], dev(x_peer(k), z, y))

    def ag2_y(k, who):
        at = w2.at[c, mine, who]
        return remote(at, at, ag2_s.at[k - 1], ag2_r.at[k - 1], dev(x, z, y_peer(k)))

    def ag3_x(k, who):
        at = w2.at[c, pl.ds(who * ZH, ZH)]
        return remote(at, at, ag3_s.at[k - 1], ag3_r.at[k - 1], dev(x_peer(k), z, y))

    def ag3_y(k, who):
        at = w2.at[c, :, who]
        return remote(at, at, ag3_s.at[k - 1], ag3_r.at[k - 1], dev(x, z, y_peer(k)))

    @pl.when(c == 0)
    def _():
        for k in range(1, NY):
            ag2_y(k, y).start()

    @pl.when(c == 1)
    def _():
        for k in range(1, NX):
            ag2_x(k, x).start()

    for step in (2, 1):
        for h in range(2):
            slot = (2 - step) * 2 + h
            arrived(kw.at[slot], k_s.at[0], k_r.at[slot])
    arrived(kw.at[4 + o], k_s.at[0], k_r.at[4 + o])
    local[0].wait()
    local[1].wait()
    local[2].wait()
    arrived(qbuf.at[o], sib_s.at[1], sib_r.at[1])
    arrived(gobuf.at[o], sib_s.at[2], sib_r.at[2])

    @pl.when(c == 0)
    def _():
        for k in range(1, NY):
            ag2_y(k, (y - k + NY) % NY).wait_recv()
        for k in range(1, NX):
            ag3_x(k, x).start()

    @pl.when(c == 1)
    def _():
        for k in range(1, NX):
            ag2_x(k, (x - k + NX) % NX).wait_recv()
        for k in range(1, NY):
            ag3_y(k, y).start()

    @pl.loop(0, 4)
    def _(u):
        t = u // 2
        g = u % 2
        kc = pl.ds(aligned(g * DH, DH), DH)
        keys = kw[pl.ds(t, 5), :, kc].reshape(5 * TOK, DH)
        grads = []
        for r in range(4):
            qc = pl.ds(aligned(g * 512 + r * DH, DH), DH)
            s = nt(qbuf[t, :, qc], keys) + bias[t]
            top = jnp.max(s, axis=1, keepdims=True)
            e = jnp.exp2((s - top) * (SCALE * math.log2(math.e)))
            inv = 1.0 / jnp.sum(e, axis=1, keepdims=True)
            pbuf[u, r * TOK : (r + 1) * TOK, :] = (e * inv).astype(BF16)
            grads.append(gobuf[t, :, qc])
        dv = tn(pbuf[u], jnp.concatenate(grads, 0))
        dvw[pl.ds(t, 5), :, kc] += dv.reshape(5, TOK, DH)

    for j in range(4):
        dvs[j] = dvw[j].astype(BF16)
    dv_sends = [
        remote(dvs.at[pl.ds((2 - k) * 2, 2)], dvr.at[k - 1], dv_s.at[k - 1], dv_r.at[k - 1], chip(-k) * 2 + c)
        for k in (1, 2)
    ]
    dv_sends[1].start()
    dv_sends[0].start()

    @pl.when(c == 0)
    def _():
        for k in range(1, NX):
            ag3_x(k, (x - k + NX) % NX).wait_recv()

    @pl.when(c == 1)
    def _():
        for k in range(1, NY):
            ag3_y(k, (y - k + NY) % NY).wait_recv()

    values = jnp.zeros((2 * TOK, HALF), F32)
    for g in range(NG):
        values = values + nn(hp[g], w2[c, g].reshape(PG, HALF))
    values = values.astype(BF16)
    vw[4] = values[:TOK]
    vw[5] = values[TOK:]
    v_sends = [
        remote(vw.at[4:6], vw.at[pl.ds((2 - k) * 2, 2)], v_s.at[k - 1], v_r.at[k - 1], chip(k) * 2 + c)
        for k in (1, 2)
    ]
    v_sends[1].start()
    v_sends[0].start()
    send_w2 = remote(w2.at[c], w2.at[c], sib_s.at[4], sib_r.at[4], sibling)
    send_w2.start()

    for k in (1, 2):
        arrived(dvr.at[k - 1], dv_s.at[k - 1], dv_r.at[k - 1])
    total = dvw[4:6] + dvr[0].astype(F32) + dvr[1].astype(F32)
    dval[...] = total.astype(BF16)
    dx[c] = dval[c]
    send_dx = remote(dval.at[o], dx.at[c], sib_s.at[5], sib_r.at[5], sibling)
    send_dx.start()

    @pl.loop(0, NG)
    def _(g):
        gw = nn(ht[g], dval[...].reshape(2 * TOK, HALF))
        gbuf[g] = gw.astype(BF16).reshape(NY, ROWS, HALF)

    def rs1_x(k):
        return remote(
            gbuf.at[pl.ds(x_peer(k) * ZH, ZH)], r1a.at[k - 1], rs1_s.at[k - 1], rs1_r.at[k - 1],
            dev(x_peer(k), z, y),
        )

    def rs1_y(k):
        return remote(
            gbuf.at[:, y_peer(k)], r1b.at[k - 1], rs1_s.at[k - 1], rs1_r.at[k - 1], dev(x, z, y_peer(k))
        )

    def rs2_y(k):
        return remote(
            s1a.at[:, y_peer(k)], r2.at[k - 1], rs2_s.at[k - 1], rs2_r.at[k - 1], dev(x, z, y_peer(k))
        )

    def rs2_x(k):
        return remote(
            s1b.at[pl.ds(x_peer(k) * ZH, ZH)], r2.at[k - 1], rs2_s.at[k - 1], rs2_r.at[k - 1],
            dev(x_peer(k), z, y),
        )

    @pl.when(c == 0)
    def _():
        for k in range(1, NX):
            rs1_x(k).start()

    @pl.when(c == 1)
    def _():
        for k in range(1, NY):
            rs1_y(k).start()

    for k in (1, 2):
        at = vw.at[pl.ds((2 - k) * 2, 2)]
        arrived(at, v_s.at[k - 1], v_r.at[k - 1])

    def path_b(t):
        @pl.loop(0, 2)
        def _(g):
            u = t * 2 + g
            kc = pl.ds(aligned(g * DH, DH), DH)
            keys = kw[pl.ds(t, 5), :, kc].reshape(5 * TOK, DH)
            vals = vw[pl.ds(t, 5), :, kc].reshape(5 * TOK, DH)
            queries = []
            for r in range(4):
                qc = pl.ds(aligned(g * 512 + r * DH, DH), DH)
                p = pbuf[u, r * TOK : (r + 1) * TOK, :]
                go = gobuf[t, :, qc]
                out = nn(p, vals).astype(BF16)
                delta = jnp.sum(go.astype(F32) * out.astype(F32), axis=1, keepdims=True)
                ds = (p.astype(F32) * (nt(go, vals) - delta)).astype(BF16)
                obuf[t, :, qc] = out
                dqbuf[t, :, qc] = (nn(ds, keys) * SCALE).astype(BF16)
                dsbuf[r * TOK : (r + 1) * TOK, :] = ds
                queries.append(qbuf[t, :, qc])
            dk = tn(dsbuf[...], jnp.concatenate(queries, 0)) * SCALE
            dkw[pl.ds(t, 5), :, kc] += dk.reshape(5, TOK, DH)

    path_b(o)
    send_o = remote(obuf.at[o], o_out.at[:, own_q], sib_s.at[6], sib_r.at[6], sibling)
    send_dq = remote(dqbuf.at[o], dq_out.at[:, own_q], sib_s.at[7], sib_r.at[7], sibling)
    send_o.start()
    send_dq.start()
    path_b(c)
    for j in range(4):
        dks[j] = dkw[j].astype(BF16)
    dk_sends = []
    for k in (2, 1):
        for t in range(2):
            i = (k - 1) * 2
            dk_sends.append(
                remote(dks.at[(2 - k) * 2 + t], dkr.at[i + c], dk_s.at[i + t], dk_r.at[i + c], chip(-k) * 2 + t)
            )
    dksib_s[...] = dkw[4 + o]
    dk_sends.append(remote(dksib_s, dksib, dk_s.at[4], dk_r.at[4], sibling))
    for copy in dk_sends:
        copy.start()
    o_out[:, own_q] = obuf[c]
    dq_out[:, own_q] = dqbuf[c]

    @pl.when(c == 0)
    def _():
        for k in range(1, NX):
            arrived(r1a.at[k - 1], rs1_s.at[k - 1], rs1_r.at[k - 1])
        part = gbuf[pl.ds(x * ZH, ZH)].astype(F32)
        for k in range(1, NX):
            part = part + r1a[k - 1].astype(F32)
        s1a[...] = part.astype(BF16)
        for k in range(1, NY):
            rs2_y(k).start()

    @pl.when(c == 1)
    def _():
        for k in range(1, NY):
            arrived(r1b.at[k - 1], rs1_s.at[k - 1], rs1_r.at[k - 1])
        part = gbuf[:, y].astype(F32)
        for k in range(1, NY):
            part = part + r1b[k - 1].astype(F32)
        s1b[...] = part.astype(BF16)
        for k in range(1, NX):
            rs2_x(k).start()

    arrived(dx.at[o], sib_s.at[5], sib_r.at[5])
    arrived(w2.at[o], sib_s.at[4], sib_r.at[4])

    @pl.loop(0, NG)
    def _(g):
        both = nt(dx[0], w2[0, g].reshape(PG, HALF)) + nt(dx[1], w2[1, g].reshape(PG, HALF))
        gh_out[:, pl.ds(aligned(g * PG, PG), PG)] = nn(both.astype(BF16), perm[...]).astype(BF16)

    @pl.when(c == 0)
    def _():
        t2[...] = s1a[:, y].astype(F32)

    @pl.when(c == 1)
    def _():
        t2[...] = s1b[pl.ds(x * ZH, ZH)].astype(F32)

    for k in range(1, NX):
        arrived(r2.at[k - 1], rs2_s.at[k - 1], rs2_r.at[k - 1])
    part = t2[...]
    for k in range(1, NX):
        part = part + r2[k - 1].astype(F32)
    part = part.reshape(NZ, 8, HALF)
    for zz in range(NZ):
        z3[zz] = jnp.concatenate([part[zz, :, :128], part[zz, :, 128:]], 0).astype(BF16)

    def rs3(k):
        z_ = (z + k) % NZ
        return remote(z3.at[z_], r3.at[z], rs3_s.at[k], rs3_r.at[k], dev(x, z_, y))

    @pl.loop(1, NZ)
    def _(k):
        rs3(k).start()

    r3[z] = z3[z]

    for i in range(4):
        arrived(dkr.at[i], dk_s.at[i], dk_r.at[i])
    arrived(dksib, dk_s.at[4], dk_r.at[4])
    gk_out[:, own_k] = (dkw[4 + c] + dkr[c].astype(F32) + dkr[2 + c].astype(F32)).astype(BF16)
    gk_out[:, oth_k] = (dksib[...] + dkr[o].astype(F32) + dkr[2 + o].astype(F32)).astype(BF16)

    @pl.loop(1, NZ)
    def _(k):
        slot = (z - k + NZ) % NZ
        remote(r3.at[slot], r3.at[slot], rs3_s.at[k], rs3_r.at[k], sibling).wait_recv()

    acc = r3[0].astype(F32)
    for zz in range(1, NZ):
        acc = acc + r3[zz].astype(F32)
    gx[c] = jnp.concatenate([acc[:8], acc[8:]], 1)
    send_gx = remote(gx.at[c], gx.at[c], sib_s.at[8], sib_r.at[8], sibling)
    send_gx.start()
    arrived(gx.at[o], sib_s.at[8], sib_r.at[8])
    both = jnp.concatenate([gx[0], gx[1]], 1)
    grad = jnp.where(c == 0, both[:4], both[4:])
    first = beta_first * m_ref[...] + (1.0 - beta_first) * grad
    second = beta_second * v_ref[...] + (1.0 - beta_second) * grad * grad
    nm_out[...] = first
    nv_out[...] = second
    first_hat = first / (1.0 - beta_first**OPT_STEP)
    second_hat = second / (1.0 - beta_second**OPT_STEP)
    w = w_ref[...]
    nw_out[...] = w - learning * (first_hat / (jnp.sqrt(second_hat) + epsilon) + decay_rate * w)

    arrived(o_out.at[:, oth_q], sib_s.at[6], sib_r.at[6])
    arrived(dq_out.at[:, oth_q], sib_s.at[7], sib_r.at[7])
    for copy in [send_w, send_hid, send_q, send_go, send_w2, send_dx, send_o, send_dq, send_gx]:
        copy.wait_send()
    for copy in k_sends + dv_sends + v_sends + dk_sends:
        copy.wait_send()

    @pl.loop(1, NZ)
    def _(k):
        ag1(k).wait_send()
        rs3(k).wait_send()

    @pl.when(c == 0)
    def _():
        for k in range(1, NX):
            ag2_y(k, y).wait_send()
            ag3_x(k, x).wait_send()
            rs1_x(k).wait_send()
            rs2_y(k).wait_send()

    @pl.when(c == 1)
    def _():
        for k in range(1, NX):
            ag2_x(k, x).wait_send()
            ag3_y(k, y).wait_send()
            rs1_y(k).wait_send()
            rs2_x(k).wait_send()


def shards(hidden, queries, key_rows, grad_out, master_value, adam_first, adam_second):
    ZH = NZ // ZL
    ROWS = ZL * 8
    PG = NY * ROWS
    NG = NX * ZH
    V = pltpu.VMEM
    DMA = pltpu.SemaphoreType.DMA
    scratch = [
        V((2, TOK, NG * PG), BF16),
        V((2, TOK, QHALF), BF16),
        V((2, TOK, QHALF), BF16),
        V((6, TOK, HALF), BF16),
        V((6, TOK, HALF), BF16),
        V((2, 4, HALF), F32),
        V((NZ, 16, 128), BF16),
        V((2, NG, NY, ROWS, HALF), BF16),
        V((2, TOK, 5 * TOK), F32),
        V((PG, PG), BF16),
        V((NG, 2 * TOK, PG), BF16),
        V((NG, PG, 2 * TOK), BF16),
        V((4, 4 * TOK, 5 * TOK), BF16),
        V((4 * TOK, 5 * TOK), BF16),
        V((6, TOK, HALF), F32),
        V((6, TOK, HALF), F32),
        V((4, TOK, HALF), BF16),
        V((2, 2, TOK, HALF), BF16),
        V((4, TOK, HALF), BF16),
        V((4, TOK, HALF), BF16),
        V((TOK, HALF), F32),
        V((TOK, HALF), F32),
        V((2, TOK, HALF), BF16),
        V((2, TOK, HALF), BF16),
        V((NG, NY, ROWS, HALF), BF16),
        V((NX - 1, ZH, NY, ROWS, HALF), BF16),
        V((NY - 1, NG, ROWS, HALF), BF16),
        V((ZH, NY, ROWS, HALF), BF16),
        V((NG, ROWS, HALF), BF16),
        V((NX - 1, ZH, ROWS, HALF), BF16),
        V((ZH, ROWS, HALF), F32),
        V((NZ, 16, 128), BF16),
        V((NZ, 16, 128), BF16),
        V((2, 8, HALF), F32),
        V((2, TOK, QHALF), BF16),
        V((2, TOK, QHALF), BF16),
        DMA((4,)),
        DMA((9,)), DMA((9,)),
        DMA((5,)), DMA((6,)),
        DMA((2,)), DMA((2,)),
        DMA((2,)), DMA((2,)),
        DMA((5,)), DMA((5,)),
        DMA((NZ,)), DMA((NZ,)),
        DMA((NX - 1,)), DMA((NX - 1,)),
        DMA((NX - 1,)), DMA((NX - 1,)),
        DMA((NX - 1,)), DMA((NX - 1,)),
        DMA((NX - 1,)), DMA((NX - 1,)),
        DMA((NZ,)), DMA((NZ,)),
    ]
    any_ = pl.BlockSpec(memory_space=pl.ANY)
    vmem = pl.BlockSpec(memory_space=pltpu.VMEM)
    outs = (queries, queries, key_rows, hidden, master_value, adam_first, adam_second)
    return pl.pallas_call(
        kernel,
        out_shape=tuple(jax.ShapeDtypeStruct(a.shape, a.dtype) for a in outs),
        in_specs=[any_, any_, any_, any_, vmem, vmem, vmem],
        out_specs=(vmem,) * 7,
        scratch_shapes=scratch,
        compiler_params=pltpu.CompilerParams(
            collective_id=0, has_side_effects=True, vmem_limit_bytes=52 * 1024 * 1024
        ),
    )(hidden, queries, key_rows, grad_out, master_value, adam_first, adam_second)


def solution(mesh):
    placed = (P("seq", None),) * 7
    return jax.shard_map(
        shards, mesh=mesh, in_specs=placed, out_specs=placed, check_vma=False
    )
```

time: 835 us -> 88 us (0.11)
  waiting for transfers between devices: 727 us -> 0 us
  Pallas kernels: 0 us -> 79.2 us
  starting transfers between devices: 40.8 us -> 0 us
  matrix products: 24.9 us -> 0 us
  between operations: 14.9 us -> 0.66 us
    unnamed x3 -> x0, waiting for transfers between devices: 503 us -> none
    all_gather x1 -> x0, waiting for transfers between devices: 197 us -> none  [shards(): weight_full = lax.all_gather(weight_low, 'seq', axis=0, tiled=True)]
    pallas_call x0 -> x1, Pallas kernels: none -> 79.2 us  [shards(): pl.pallas_call(kernel, out_shape=tuple((jax.ShapeDtypeStruct(a.shape, a.d...]
    ppermute x16 -> x0, starting transfers between devices: 40.7 us -> none  [passed_along(): return lax.ppermute(block, axis, route)]
    ppermute x16 -> x0, waiting for transfers between devices: 26.7 us -> none  [passed_along(): return lax.ppermute(block, axis, route)]
    dot_general x23 -> x0, matrix products: 15.9 us -> none  [the longest x4 5.02 us: attend_block(): jnp.einsum('trs,sd->trd', dscore, key_group, preferred_element_type=jnp.f...]
    sub x4 -> x0, matrix products: 9.04 us -> none  [attend_block(): expd = jnp.exp(scores - top)]
  transfers between devices with their start and end apart: 18 -> 0, of which waited for: 11 -> 0; matrix products, arithmetic and copies ran while one was open for 1% -> 0% of each run, Pallas kernels for 0% -> 0%
where the time goes in v1:
time: 88 us; the launch traced here: 87.7 us
  Pallas kernels  79.2 us (90%)
  local copies, waits for them, and re-layouts  7.82 us (9%)
    pallas_call x1, Pallas kernels, shards(): pl.pallas_call(kernel, out_shape=tuple((jax.ShapeDtypeStruct(a.shape, a.d...  79.2 us
    unnamed x15, local copies, waits for them, and re-layouts  7.82 us

profile of v1, /device:TPU:1, one launch (start us, length us, event | category | flops | bytes accessed | tf_op | source)
XLA Modules:
  0.0 87.7 jit_solution(4050260983727092602)
XLA Ops:
  0.6 0.0 copy-start
  0.6 0.9 %copy-done = bf16[128,512]{1,0:T(8,128)(2,1)S(1)} copy-done((bf16[128,512]{1,0:T(8,128)(2,1)S(1)}, bf16[128,512]{1,0:T(8,128)(2,1)}, u32[]{:S(2)}) %copy-start) | copy-done | bytes 131096
  1.5 0.0 copy-start.1
  1.5 0.7 copy-done.1
  2.2 0.0 copy-start.2
  2.2 0.7 copy-done.2
  2.9 0.0 copy-start.3
  2.9 0.7 copy-done.3
  3.6 79.2 %shard_map.126 = (bf16[128,2048]{1,0:T(8,128)(2,1)S(1)}, bf16[128,2048]{1,0:T(8,128)(2,1)S(1)}, bf16[128,512]{1,0:T(8,128)(2,1)S(1)}, bf16[128,2048]{1,0:T(8,128...) custom-call(bf16[128,2048]{1,0:T(8,128)(2,1)} %hid_ref.1, bf16[128,2048]{1,0:T(8,128)(2,1)} %q_ref.1, ...), custom_call_target="tpu_custom_call" | custom-call | tf_op jit(solution)/shard_map/pallas_call | solution.py:570
  82.8 0.8 copy.21
  83.6 0.8 copy.22
  84.4 0.7 copy.23
  85.1 0.8 copy.24
  85.9 0.6 copy.25
  86.5 0.6 copy.26
  87.1 0.6 copy.27
Async XLA Ops:
  0.6 0.9 %copy-start = (bf16[128,512]{1,0:T(8,128)(2,1)S(1)}, bf16[128,512]{1,0:T(8,128)(2,1)}, u32[]{:S(2)}) copy-start(bf16[128,512]{1,0:T(8,128)(2,1)} %k_ref.1) | copy-start | bytes 393220
  1.5 0.7 copy-start.1
  2.2 0.7 copy-start.2
  2.9 0.7 copy-start.3

commit v2 on v1

v2 whole, which is shorter than its diff:
```python
import math

import jax
import jax.numpy as jnp
from jax import lax
from jax.experimental import pallas as pl
from jax.experimental.pallas import tpu as pltpu
from jax.sharding import PartitionSpec as P

HQ = 16
HK = 4
DH = 128
WINDOW = 512
OPT_STEP = 10
TOK = 128
SCALE = 1.0 / math.sqrt(DH)

beta_first = 0.9
beta_second = 0.95
learning = 0.001
decay_rate = 0.1
epsilon = 1e-08

F32 = jnp.float32
BF16 = jnp.bfloat16
MESH = pl.DeviceIdType.MESH

NX, NZ, NY = 4, 16, 4
ZL = 8
HALF = 256
QHALF = 1024


def nt(a, b):
    return lax.dot_general(a, b, (((1,), (1,)), ((), ())), preferred_element_type=F32)


def nn(a, b):
    return lax.dot_general(a, b, (((1,), (0,)), ((), ())), preferred_element_type=F32)


def tn(a, b):
    return lax.dot_general(a, b, (((0,), (0,)), ((), ())), preferred_element_type=F32)


def aligned(value, multiple):
    return pl.multiple_of(value, multiple)


def kernel(
    hid_ref, q_ref, k_ref, go_ref, w_ref, m_ref, v_ref,
    o_out, dq_out, gk_out, gh_out, nw_out, nm_out, nv_out,
    hbuf, qbuf, gobuf, kw, vw, wsib, wz, w2, bias, perm, hp, ht, pbuf, dsbuf,
    dvw, dkw, dvs, dvr, dks, dkr, dksib, dksib_s, dval, dx,
    gbuf, r1a, r1b, s1a, s1b, r2, t2, z3, r3, gx, obuf, dqbuf, adam, ghbuf,
    loc, sib_s, sib_r, k_s, k_r, v_s, v_r, dv_s, dv_r, dk_s, dk_r,
    ag1_s, ag1_r, ag2_s, ag2_r, ag3_s, ag3_r, rs1_s, rs1_r, rs2_s, rs2_r, rs3_s, rs3_r,
):
    ZH = NZ // ZL
    ROWS = ZL * 8
    PG = NY * ROWS
    NG = NX * ZH
    NCHIP = NX * NZ * NY
    d = lax.axis_index("seq")
    c = d % 2
    o = 1 - c
    n = d // 2
    y = n % NY
    z = (n // NY) % NZ
    x = n // (NY * NZ)

    def chip(step):
        return (n + step + NCHIP) % NCHIP

    def dev(x_, z_, y_):
        return ((x_ * NZ + z_) * NY + y_) * 2 + c

    sibling = n * 2 + o

    def remote(src, dst, ssem, rsem, device):
        return pltpu.make_async_remote_copy(
            src_ref=src, dst_ref=dst, send_sem=ssem, recv_sem=rsem,
            device_id=(device,), device_id_type=MESH,
        )

    def x_peer(k):
        return (x + k) % NX

    def y_peer(k):
        return (y + k) % NY

    pending = []

    def later(key, wait):
        pending.append((key, wait))

    def now(key):
        for item in [p for p in pending if p[0] == key]:
            item[1]()
            pending.remove(item)

    def go(copy, key):
        copy.start()
        later(key, copy.wait_recv)
        later("sent", copy.wait_send)

    def arrived(dst, ssem, rsem):
        remote(dst, dst, ssem, rsem, sibling).wait_recv()

    def on_core(which, act):
        @pl.when(c == which)
        def _():
            act()

    def along(key, zero, one):
        for which, (send, wait) in ((0, zero), (1, one)):
            def start(send=send):
                for k in (2, 1, 3) if NX == 4 else range(1, NX):
                    send(k).start()

            def got(wait=wait):
                for k in range(1, NX):
                    wait(k).wait_recv()

            def left(send=send):
                for k in range(1, NX):
                    send(k).wait_send()

            on_core(which, start)
            later(key, lambda which=which, act=got: on_core(which, act))
            later("sent", lambda which=which, act=left: on_core(which, act))

    def ring(key, send, wait):
        @pl.loop(0, NZ - 1)
        def _(i):
            far = (i + 1) // 2
            send(NZ // 2 + jnp.where(i % 2 == 0, far, -far)).start()

        def got():
            @pl.loop(1, NZ)
            def _(k):
                wait(k).wait_recv()

        def left():
            @pl.loop(1, NZ)
            def _(k):
                send(k).wait_send()

        later(key, got)
        later("sent", left)

    barrier = pltpu.get_barrier_semaphore()

    def greet(device):
        pl.semaphore_signal(barrier, inc=1, device_id=(device,), device_id_type=MESH)

    @pl.loop(0, NZ - 1)
    def _(i):
        far = (i + 1) // 2
        greet(dev(x, (z + NZ // 2 + jnp.where(i % 2 == 0, far, -far)) % NZ, y))

    for k in range(1, NX):
        greet(dev(x_peer(k), z, y))
    for k in range(1, NY):
        greet(dev(x, z, y_peer(k)))
    for step in (-2, -1, 1, 2):
        for h in range(2):
            greet(chip(step) * 2 + h)
    greet(sibling)

    own_q = pl.ds(aligned(c * QHALF, QHALF), QHALF)
    oth_q = pl.ds(aligned(o * QHALF, QHALF), QHALF)
    own_k = pl.ds(aligned(c * HALF, HALF), HALF)
    oth_k = pl.ds(aligned(o * HALF, HALF), HALF)

    for i, (key, src, dst) in enumerate(
        (
            ("w", w_ref.at[:, own_k], wsib.at[c]),
            ("k", k_ref.at[:, own_k], kw.at[4 + c]),
            ("q", q_ref.at[:, own_q], qbuf.at[c]),
            ("q", go_ref.at[:, own_q], gobuf.at[c]),
            ("hid", hid_ref, hbuf.at[c]),
            ("adam", w_ref, adam.at[0]),
            ("adam", m_ref, adam.at[1]),
            ("adam", v_ref, adam.at[2]),
        )
    ):
        copy = pltpu.make_async_copy(src, dst, loc.at[i])
        copy.start()
        later(key, copy.wait)

    row = lax.broadcasted_iota(jnp.int32, (TOK, 5 * TOK), 0)
    col = lax.broadcasted_iota(jnp.int32, (TOK, 5 * TOK), 1)
    relative = row + WINDOW - col
    for t in range(2):
        first = (d - c + t) * TOK - WINDOW
        allowed = (relative >= 0) & (relative < WINDOW) & (col + first >= 0)
        bias[t] = jnp.where(allowed, 0.0, -1e30).astype(F32)
    prow = lax.broadcasted_iota(jnp.int32, (PG, PG), 0)
    pcol = lax.broadcasted_iota(jnp.int32, (PG, PG), 1)
    source = ((prow % ROWS) // 8) * (NY * 8) + (prow // ROWS) * 8 + prow % 8
    perm[...] = jnp.where(source == pcol, 1.0, 0.0).astype(BF16)
    dvw[...] = jnp.zeros(dvw.shape, F32)
    dkw[...] = jnp.zeros(dkw.shape, F32)

    pl.semaphore_wait(barrier, 1 + 8 + (NX - 1) + (NY - 1) + (NZ - 1))

    go(remote(w_ref.at[:, oth_k], wsib.at[c], sib_s.at[0], sib_r.at[0], sibling), "w")
    go(remote(k_ref.at[:, oth_k], kw.at[4 + c], k_s.at[0], k_r.at[4 + c], sibling), "none")
    for i, (step, h) in enumerate(((1, 0), (1, 1), (2, 0), (2, 1))):
        slot = (2 - step) * 2 + c
        go(
            remote(
                k_ref.at[:, h * HALF : (h + 1) * HALF], kw.at[slot], k_s.at[1 + i], k_r.at[slot],
                chip(step) * 2 + h,
            ),
            "none",
        )
    pending[:] = [p for p in pending if p[0] != "none"]

    def keys_in():
        arrived(kw.at[4 + o], k_s.at[0], k_r.at[4 + o])
        for slot in (2, 3, 0, 1):
            arrived(kw.at[slot], k_s.at[0], k_r.at[slot])

    later("k", keys_in)
    go(remote(q_ref.at[:, oth_q], qbuf.at[c], sib_s.at[1], sib_r.at[1], sibling), "q")
    go(remote(go_ref.at[:, oth_q], gobuf.at[c], sib_s.at[2], sib_r.at[2], sibling), "q")
    go(remote(hid_ref, hbuf.at[c], sib_s.at[3], sib_r.at[3], sibling), "hid")

    now("w")
    block = jnp.concatenate([wsib[0], wsib[1]], 0)
    wz[z] = jnp.concatenate([block[:, :128], block[:, 128:]], 0).astype(BF16)

    def ag1(k):
        return remote(wz.at[z], wz.at[z], ag1_s.at[k], ag1_r.at[k], dev(x, (z + k) % NZ, y))

    def ag1_in(k):
        slot = (z - k + NZ) % NZ
        return remote(wz.at[slot], wz.at[slot], ag1_s.at[k], ag1_r.at[k], sibling)

    ring("ag1", ag1, ag1_in)

    def ag2_x(k, who):
        at = w2.at[c, pl.ds(who * ZH, ZH), y]
        return remote(at, at, ag2_s.at[k - 1], ag2_r.at[k - 1], dev(x_peer(k), z, y))

    def ag2_y(k, who):
        at = w2.at[c, pl.ds(x * ZH, ZH), who]
        return remote(at, at, ag2_s.at[k - 1], ag2_r.at[k - 1], dev(x, z, y_peer(k)))

    def ag3_x(k, who):
        at = w2.at[c, pl.ds(who * ZH, ZH)]
        return remote(at, at, ag3_s.at[k - 1], ag3_r.at[k - 1], dev(x_peer(k), z, y))

    def ag3_y(k, who):
        at = w2.at[c, :, who]
        return remote(at, at, ag3_s.at[k - 1], ag3_r.at[k - 1], dev(x, z, y_peer(k)))

    def gather_second():
        now("ag1")
        for zh in range(ZH):
            rows = []
            for zl in range(ZL):
                block = wz[zh * ZL + zl].astype(F32)
                rows.append(jnp.concatenate([block[:8], block[8:]], 1))
            w2[c, x * ZH + zh, y] = jnp.concatenate(rows, 0).astype(BF16)
        along(
            "ag2",
            (lambda k: ag2_y(k, y), lambda k: ag2_y(k, (y - k + NY) % NY)),
            (lambda k: ag2_x(k, x), lambda k: ag2_x(k, (x - k + NX) % NX)),
        )

    def gather_third():
        now("ag2")
        along(
            "ag3",
            (lambda k: ag3_x(k, x), lambda k: ag3_x(k, (x - k + NX) % NX)),
            (lambda k: ag3_y(k, y), lambda k: ag3_y(k, (y - k + NY) % NY)),
        )

    def path_a(t, g):
        keys = kw[pl.ds(t, 5), :, g * DH : (g + 1) * DH].reshape(5 * TOK, DH)
        grads = []
        for r in range(4):
            qc = slice(g * 512 + r * DH, g * 512 + (r + 1) * DH)
            s = nt(qbuf[t, :, qc], keys) + bias[t]
            top = jnp.max(s, axis=1, keepdims=True)
            e = jnp.exp2((s - top) * (SCALE * math.log2(math.e)))
            inv = 1.0 / jnp.sum(e, axis=1, keepdims=True)
            pbuf[t * 2 + g, r * TOK : (r + 1) * TOK, :] = (e * inv).astype(BF16)
            grads.append(gobuf[t, :, qc])
        dv = tn(pbuf[t * 2 + g], jnp.concatenate(grads, 0))
        dvw[pl.ds(t, 5), :, g * DH : (g + 1) * DH] += dv.reshape(5, TOK, DH)

    now("k")
    now("q")
    for g in range(2):
        @pl.loop(0, 2)
        def _(t):
            path_a(t, g)

        for j in range(4):
            dvs[g, j] = dvw[j, :, g * DH : (g + 1) * DH].astype(BF16)
        for k in (1, 2):
            i = g * 2 + k - 1
            go(
                remote(dvs.at[g, pl.ds((2 - k) * 2, 2)], dvr.at[i], dv_s.at[i], dv_r.at[i], chip(-k) * 2 + c),
                "dv",
            )
        if g == 0:
            gather_second()

    now("hid")

    def features(low, high):
        @pl.loop(low, high)
        def _(g):
            cols = pl.ds(aligned(g * PG, PG), PG)
            both = jnp.concatenate([hbuf[0, :, cols], hbuf[1, :, cols]], 0)
            hp[g] = nt(both, perm[...]).astype(BF16)
            ht[g] = nt(perm[...], both).astype(BF16)

    features(0, NG // 2)
    gather_third()
    features(NG // 2, NG)

    now("dv")
    for g in range(2):
        cols = slice(g * DH, (g + 1) * DH)
        total = dvw[4:6, :, cols] + dvr[g * 2].astype(F32) + dvr[g * 2 + 1].astype(F32)
        dval[:, :, cols] = total.astype(BF16)
    dx[c] = dval[c]
    go(remote(dval.at[o], dx.at[c], sib_s.at[5], sib_r.at[5], sibling), "dx")

    @pl.loop(0, NG)
    def _(g):
        gw = nn(ht[g], dval[...].reshape(2 * TOK, HALF))
        gbuf[g] = gw.astype(BF16).reshape(NY, ROWS, HALF)

    def rs1_x(k):
        return remote(
            gbuf.at[pl.ds(x_peer(k) * ZH, ZH)], r1a.at[k - 1], rs1_s.at[k - 1], rs1_r.at[k - 1],
            dev(x_peer(k), z, y),
        )

    def rs1_y(k):
        return remote(
            gbuf.at[:, y_peer(k)], r1b.at[k - 1], rs1_s.at[k - 1], rs1_r.at[k - 1], dev(x, z, y_peer(k))
        )

    def rs2_y(k):
        return remote(
            s1a.at[:, y_peer(k)], r2.at[k - 1], rs2_s.at[k - 1], rs2_r.at[k - 1], dev(x, z, y_peer(k))
        )

    def rs2_x(k):
        return remote(
            s1b.at[pl.ds(x_peer(k) * ZH, ZH)], r2.at[k - 1], rs2_s.at[k - 1], rs2_r.at[k - 1],
            dev(x_peer(k), z, y),
        )

    along("rs1", (rs1_x, rs1_x), (rs1_y, rs1_y))

    now("ag3")
    values = jnp.zeros((2 * TOK, HALF), F32)
    for g in range(NG):
        values = values + nn(hp[g], w2[c, g].reshape(PG, HALF))
    values = values.astype(BF16)
    vw[4] = values[:TOK]
    vw[5] = values[TOK:]
    for k in (1, 2):
        go(
            remote(vw.at[4:6], vw.at[pl.ds((2 - k) * 2, 2)], v_s.at[k - 1], v_r.at[k - 1], chip(k) * 2 + c),
            "none",
        )
        at = vw.at[pl.ds((2 - k) * 2, 2)]
        later("v", lambda at=at, k=k: arrived(at, v_s.at[k - 1], v_r.at[k - 1]))
    pending[:] = [p for p in pending if p[0] != "none"]
    go(remote(w2.at[c], w2.at[c], sib_s.at[4], sib_r.at[4], sibling), "none")
    pending[:] = [p for p in pending if p[0] != "none"]
    later("w2", lambda: arrived(w2.at[o], sib_s.at[4], sib_r.at[4]))

    now("dx")
    now("w2")

    @pl.loop(0, NG)
    def _(g):
        both = nt(dx[0], w2[0, g].reshape(PG, HALF)) + nt(dx[1], w2[1, g].reshape(PG, HALF))
        ghbuf[:, pl.ds(aligned(g * PG, PG), PG)] = nn(both.astype(BF16), perm[...]).astype(BF16)

    copy = pltpu.make_async_copy(ghbuf, gh_out, loc.at[10])
    copy.start()
    later("sent", copy.wait)

    now("rs1")

    def sum_zero():
        part = gbuf[pl.ds(x * ZH, ZH)].astype(F32)
        for k in range(1, NX):
            part = part + r1a[k - 1].astype(F32)
        s1a[...] = part.astype(BF16)
        t2[...] = s1a[:, y].astype(F32)

    def sum_one():
        part = gbuf[:, y].astype(F32)
        for k in range(1, NY):
            part = part + r1b[k - 1].astype(F32)
        s1b[...] = part.astype(BF16)
        t2[...] = s1b[pl.ds(x * ZH, ZH)].astype(F32)

    on_core(0, sum_zero)
    on_core(1, sum_one)
    along("rs2", (rs2_y, rs2_y), (rs2_x, rs2_x))

    def rs3(k):
        z_ = (z + k) % NZ
        return remote(z3.at[z_], r3.at[z], rs3_s.at[k], rs3_r.at[k], dev(x, z_, y))

    def rs3_in(k):
        slot = (z - k + NZ) % NZ
        return remote(r3.at[slot], r3.at[slot], rs3_s.at[k], rs3_r.at[k], sibling)

    def scatter_third():
        now("rs2")
        part = t2[...]
        for k in range(1, NX):
            part = part + r2[k - 1].astype(F32)
        part = part.reshape(NZ, 8, HALF)
        for zz in range(NZ):
            z3[zz] = jnp.concatenate([part[zz, :, :128], part[zz, :, 128:]], 0).astype(BF16)
        ring("rs3", rs3, rs3_in)
        r3[z] = z3[z]

    def path_b(t, g):
        keys = kw[pl.ds(t, 5), :, g * DH : (g + 1) * DH].reshape(5 * TOK, DH)
        vals = vw[pl.ds(t, 5), :, g * DH : (g + 1) * DH].reshape(5 * TOK, DH)
        queries = []
        for r in range(4):
            qc = slice(g * 512 + r * DH, g * 512 + (r + 1) * DH)
            p = pbuf[t * 2 + g, r * TOK : (r + 1) * TOK, :]
            grad = gobuf[t, :, qc]
            out = nn(p, vals).astype(BF16)
            delta = jnp.sum(grad.astype(F32) * out.astype(F32), axis=1, keepdims=True)
            ds = (p.astype(F32) * (nt(grad, vals) - delta)).astype(BF16)
            obuf[t, :, qc] = out
            dqbuf[t, :, qc] = (nn(ds, keys) * SCALE).astype(BF16)
            dsbuf[r * TOK : (r + 1) * TOK, :] = ds
            queries.append(qbuf[t, :, qc])
        dk = tn(dsbuf[...], jnp.concatenate(queries, 0)) * SCALE
        dkw[pl.ds(t, 5), :, g * DH : (g + 1) * DH] += dk.reshape(5, TOK, DH)

    now("v")
    for g in range(2):
        cols = slice(g * DH, (g + 1) * DH)

        @pl.loop(0, 2)
        def _(t):
            path_b(t, g)

        if g == 0:
            scatter_third()
        for j in range(4):
            dks[g, j] = dkw[j, :, cols].astype(BF16)
        dksib_s[g] = dkw[4 + o, :, cols]
        for k in (1, 2):
            for t in range(2):
                i = g * 4 + (k - 1) * 2
                copy = remote(
                    dks.at[g, (2 - k) * 2 + t], dkr.at[i + c], dk_s.at[i + t], dk_r.at[i + c], chip(-k) * 2 + t
                )
                copy.start()
                later("sent", copy.wait_send)
        go(remote(dksib_s.at[g], dksib.at[g], dk_s.at[8 + g], dk_r.at[8 + g], sibling), "dk")
        for i in range(g * 4, g * 4 + 4):
            later("dk", lambda i=i: arrived(dkr.at[i], dk_s.at[i], dk_r.at[i]))

    for i, (buf, out) in enumerate(((obuf, o_out), (dqbuf, dq_out))):
        go(remote(buf.at[o], out.at[:, own_q], sib_s.at[6 + i], sib_r.at[6 + i], sibling), "none")
        pending[:] = [p for p in pending if p[0] != "none"]
        at = out.at[:, oth_q]
        later("out", lambda i=i, at=at: arrived(at, sib_s.at[6 + i], sib_r.at[6 + i]))
        copy = pltpu.make_async_copy(buf.at[c], out.at[:, own_q], loc.at[8 + i])
        copy.start()
        later("sent", copy.wait)

    now("dk")
    for g in range(2):
        own = dkw[4 + c, :, g * DH : (g + 1) * DH]
        own = own + dkr[g * 4 + c].astype(F32) + dkr[g * 4 + 2 + c].astype(F32)
        oth = dksib[g] + dkr[g * 4 + o].astype(F32) + dkr[g * 4 + 2 + o].astype(F32)
        gk_out[:, pl.ds(aligned(c * HALF + g * DH, DH), DH)] = own.astype(BF16)
        gk_out[:, pl.ds(aligned(o * HALF + g * DH, DH), DH)] = oth.astype(BF16)

    now("rs3")
    acc = r3[0].astype(F32)
    for zz in range(1, NZ):
        acc = acc + r3[zz].astype(F32)
    gx[c] = jnp.concatenate([acc[:8], acc[8:]], 1)
    go(remote(gx.at[c], gx.at[c], sib_s.at[8], sib_r.at[8], sibling), "none")
    pending[:] = [p for p in pending if p[0] != "none"]
    now("adam")
    arrived(gx.at[o], sib_s.at[8], sib_r.at[8])
    both = jnp.concatenate([gx[0], gx[1]], 1)
    grad = jnp.where(c == 0, both[:4], both[4:])
    first = beta_first * adam[1] + (1.0 - beta_first) * grad
    second = beta_second * adam[2] + (1.0 - beta_second) * grad * grad
    nm_out[...] = first
    nv_out[...] = second
    first_hat = first / (1.0 - beta_first**OPT_STEP)
    second_hat = second / (1.0 - beta_second**OPT_STEP)
    w = adam[0]
    nw_out[...] = w - learning * (first_hat / (jnp.sqrt(second_hat) + epsilon) + decay_rate * w)

    for key, wait in pending:
        wait()


def settle(*refs):
    sems = refs[-1]
    copies = [pltpu.make_async_copy(refs[i], refs[7 + i], sems.at[i]) for i in range(7)]
    for copy in copies:
        copy.start()
    for copy in copies:
        copy.wait()


def shards(hidden, queries, key_rows, grad_out, master_value, adam_first, adam_second):
    ZH = NZ // ZL
    ROWS = ZL * 8
    PG = NY * ROWS
    NG = NX * ZH
    V = pltpu.VMEM
    DMA = pltpu.SemaphoreType.DMA
    scratch = [
        V((2, TOK, NG * PG), BF16),
        V((2, TOK, QHALF), BF16),
        V((2, TOK, QHALF), BF16),
        V((6, TOK, HALF), BF16),
        V((6, TOK, HALF), BF16),
        V((2, 4, HALF), F32),
        V((NZ, 16, 128), BF16),
        V((2, NG, NY, ROWS, HALF), BF16),
        V((2, TOK, 5 * TOK), F32),
        V((PG, PG), BF16),
        V((NG, 2 * TOK, PG), BF16),
        V((NG, PG, 2 * TOK), BF16),
        V((4, 4 * TOK, 5 * TOK), BF16),
        V((4 * TOK, 5 * TOK), BF16),
        V((6, TOK, HALF), F32),
        V((6, TOK, HALF), F32),
        V((2, 4, TOK, DH), BF16),
        V((4, 2, TOK, DH), BF16),
        V((2, 4, TOK, DH), BF16),
        V((8, TOK, DH), BF16),
        V((2, TOK, DH), F32),
        V((2, TOK, DH), F32),
        V((2, TOK, HALF), BF16),
        V((2, TOK, HALF), BF16),
        V((NG, NY, ROWS, HALF), BF16),
        V((NX - 1, ZH, NY, ROWS, HALF), BF16),
        V((NY - 1, NG, ROWS, HALF), BF16),
        V((ZH, NY, ROWS, HALF), BF16),
        V((NG, ROWS, HALF), BF16),
        V((NX - 1, ZH, ROWS, HALF), BF16),
        V((ZH, ROWS, HALF), F32),
        V((NZ, 16, 128), BF16),
        V((NZ, 16, 128), BF16),
        V((2, 8, HALF), F32),
        V((2, TOK, QHALF), BF16),
        V((2, TOK, QHALF), BF16),
        V((3, 4, 2 * HALF), F32),
        V((TOK, NG * PG), BF16),
        DMA((11,)),
        DMA((9,)), DMA((9,)),
        DMA((5,)), DMA((6,)),
        DMA((2,)), DMA((2,)),
        DMA((4,)), DMA((4,)),
        DMA((10,)), DMA((10,)),
        DMA((NZ,)), DMA((NZ,)),
        DMA((NX - 1,)), DMA((NX - 1,)),
        DMA((NX - 1,)), DMA((NX - 1,)),
        DMA((NX - 1,)), DMA((NX - 1,)),
        DMA((NX - 1,)), DMA((NX - 1,)),
        DMA((NZ,)), DMA((NZ,)),
    ]
    hbm = pl.BlockSpec(memory_space=pltpu.HBM)
    anywhere = pl.BlockSpec(memory_space=pl.ANY)
    vmem = pl.BlockSpec(memory_space=pltpu.VMEM)
    outs = (queries, queries, key_rows, hidden, master_value, adam_first, adam_second)
    shapes = tuple(jax.ShapeDtypeStruct(a.shape, a.dtype) for a in outs)
    results = pl.pallas_call(
        kernel,
        out_shape=shapes,
        in_specs=[hbm] * 7,
        out_specs=(anywhere, anywhere, vmem, anywhere, vmem, vmem, vmem),
        scratch_shapes=scratch,
        compiler_params=pltpu.CompilerParams(
            collective_id=0, has_side_effects=True, vmem_limit_bytes=52 * 1024 * 1024
        ),
    )(
        *(
            pltpu.with_memory_space_constraint(a, pltpu.HBM)
            for a in (hidden, queries, key_rows, grad_out, master_value, adam_first, adam_second)
        )
    )
    return pl.pallas_call(
        settle,
        out_shape=shapes,
        in_specs=[anywhere] * 7,
        out_specs=(hbm,) * 7,
        scratch_shapes=[DMA((7,))],
        compiler_params=pltpu.CompilerParams(vmem_limit_bytes=2 * 1024 * 1024),
    )(*results)


def solution(mesh):
    placed = (P("seq", None),) * 7
    return jax.shard_map(
        shards, mesh=mesh, in_specs=placed, out_specs=placed, check_vma=False
    )
```

time: 88 us -> 76.5 us (0.87)
  local copies, waits for them, and re-layouts: 7.82 us -> 0 us
  Pallas kernels: 79.2 us -> 75.8 us
    unnamed x15 -> x0, local copies, waits for them, and re-layouts: 7.82 us -> none
    pallas_call x1 -> x2, Pallas kernels: 79.2 us -> 75.8 us  [the longest x1 74.5 us: shards(): pl.pallas_call(kernel, out_shape=shapes, in_specs=[hbm] * 7, out_specs=(a...]
where the time goes in v2:
time: 76.5 us; the launch traced here: 76.4 us
  Pallas kernels  75.8 us (99%)
    pallas_call x1, Pallas kernels, shards(): pl.pallas_call(kernel, out_shape=shapes, in_specs=[hbm] * 7, out_specs=(a...  74.5 us

profile of v2, /device:TPU:1, one launch (start us, length us, event | category | flops | bytes accessed | tf_op | source)
XLA Modules:
  0.0 76.4 jit_solution(14790493438083247654)
XLA Ops:
  0.6 74.5 %shard_map.126 = (bf16[128,2048]{1,0:T(8,128)(2,1)S(1)}, bf16[128,2048]{1,0:T(8,128)(2,1)S(1)}, bf16[128,512]{1,0:T(8,128)(2,1)S(1)}, bf16[128,2048]{1,0:T(8,128...) custom-call(bf16[128,2048]{1,0:T(8,128)(2,1)} %hid_ref.1, bf16[128,2048]{1,0:T(8,128)(2,1)} %q_ref.1, ...), custom_call_target="tpu_custom_call" | custom-call | tf_op jit(solution)/shard_map/pallas_call | solution.py:592
  75.1 1.3 %shard_map.127 = (bf16[128,2048]{1,0:T(8,128)(2,1)}, bf16[128,2048]{1,0:T(8,128)(2,1)}, bf16[128,512]{1,0:T(8,128)(2,1)}, bf16[128,2048]{1,0:T(8,128)(2,1)}, f32...) custom-call(bf16[128,2048]{1,0:T(8,128)(2,1)S(1)} %get-tuple-element.14.refs_0_, ...), custom_call_target="tpu_custom_call" | custom-call | tf_op jit(solution)/shard_map/pallas_call | solution.py:607

commit v3 on v2

--- a/solution.py
+++ b/solution.py
@@ -1,3 +1,4 @@
+import functools
 import math
 
 import jax
@@ -249,13 +250,22 @@
         at = w2.at[c, pl.ds(x * ZH, ZH), who]
         return remote(at, at, ag2_s.at[k - 1], ag2_r.at[k - 1], dev(x, z, y_peer(k)))
 
-    def ag3_x(k, who):
-        at = w2.at[c, pl.ds(who * ZH, ZH)]
-        return remote(at, at, ag3_s.at[k - 1], ag3_r.at[k - 1], dev(x_peer(k), z, y))
-
-    def ag3_y(k, who):
-        at = w2.at[c, :, who]
-        return remote(at, at, ag3_s.at[k - 1], ag3_r.at[k - 1], dev(x, z, y_peer(k)))
+    def ag3_x(j, k, who):
+        at = w2.at[c, pl.ds(who * ZH, ZH), (y - j + NY) % NY]
+        i = j * (NX - 1) + k - 1
+        return remote(at, at, ag3_s.at[i], ag3_r.at[i], dev(x_peer(k), z, y))
+
+    def ag3_y(j, k, who):
+        at = w2.at[c, pl.ds(((x - j + NX) % NX) * ZH, ZH), who]
+        i = j * (NX - 1) + k - 1
+        return remote(at, at, ag3_s.at[i], ag3_r.at[i], dev(x, z, y_peer(k)))
+
+    def gather_third(j):
+        along(
+            "ag3",
+            (lambda k: ag3_x(j, k, x), lambda k: ag3_x(j, k, (x - k + NX) % NX)),
+            (lambda k: ag3_y(j, k, y), lambda k: ag3_y(j, k, (y - k + NY) % NY)),
+        )
 
     def gather_second():
         now("ag1")
@@ -270,14 +280,7 @@
             (lambda k: ag2_y(k, y), lambda k: ag2_y(k, (y - k + NY) % NY)),
             (lambda k: ag2_x(k, x), lambda k: ag2_x(k, (x - k + NX) % NX)),
         )
-
-    def gather_third():
-        now("ag2")
-        along(
-            "ag3",
-            (lambda k: ag3_x(k, x), lambda k: ag3_x(k, (x - k + NX) % NX)),
-            (lambda k: ag3_y(k, y), lambda k: ag3_y(k, (y - k + NY) % NY)),
-        )
+        gather_third(0)
 
     def path_a(t, g):
         keys = kw[pl.ds(t, 5), :, g * DH : (g + 1) * DH].reshape(5 * TOK, DH)
@@ -293,6 +296,7 @@
         dv = tn(pbuf[t * 2 + g], jnp.concatenate(grads, 0))
         dvw[pl.ds(t, 5), :, g * DH : (g + 1) * DH] += dv.reshape(5, TOK, DH)
 
+    gather_second()
     now("k")
     now("q")
     for g in range(2):
@@ -306,48 +310,55 @@
             i = g * 2 + k - 1
             go(
                 remote(dvs.at[g, pl.ds((2 - k) * 2, 2)], dvr.at[i], dv_s.at[i], dv_r.at[i], chip(-k) * 2 + c),
-                "dv",
+                "dv%d" % g,
             )
-        if g == 0:
-            gather_second()
+
+    now("ag2")
+    for j in range(1, NY):
+        gather_third(j)
 
     now("hid")
 
-    def features(low, high):
-        @pl.loop(low, high)
-        def _(g):
-            cols = pl.ds(aligned(g * PG, PG), PG)
-            both = jnp.concatenate([hbuf[0, :, cols], hbuf[1, :, cols]], 0)
-            hp[g] = nt(both, perm[...]).astype(BF16)
-            ht[g] = nt(perm[...], both).astype(BF16)
-
-    features(0, NG // 2)
-    gather_third()
-    features(NG // 2, NG)
-
-    now("dv")
+    @pl.loop(0, NG)
+    def _(g):
+        cols = pl.ds(aligned(g * PG, PG), PG)
+        both = jnp.concatenate([hbuf[0, :, cols], hbuf[1, :, cols]], 0)
+        hp[g] = nt(both, perm[...]).astype(BF16)
+        ht[g] = nt(perm[...], both).astype(BF16)
+
+    def rs1_x(g, k):
+        low = slice(g * DH, (g + 1) * DH)
+        i = g * (NX - 1) + k - 1
+        return remote(
+            gbuf.at[pl.ds(x_peer(k) * ZH, ZH), :, :, low], r1a.at[k - 1, :, :, :, low], rs1_s.at[i], rs1_r.at[i],
+            dev(x_peer(k), z, y),
+        )
+
+    def rs1_y(g, k):
+        low = slice(g * DH, (g + 1) * DH)
+        i = g * (NX - 1) + k - 1
+        return remote(
+            gbuf.at[:, y_peer(k), :, low], r1b.at[k - 1, :, :, low], rs1_s.at[i], rs1_r.at[i],
+            dev(x, z, y_peer(k)),
+        )
+
     for g in range(2):
-        cols = slice(g * DH, (g + 1) * DH)
-        total = dvw[4:6, :, cols] + dvr[g * 2].astype(F32) + dvr[g * 2 + 1].astype(F32)
-        dval[:, :, cols] = total.astype(BF16)
+        now("dv%d" % g)
+        low = slice(g * DH, (g + 1) * DH)
+        total = dvw[4:6, :, low] + dvr[g * 2].astype(F32) + dvr[g * 2 + 1].astype(F32)
+        dval[:, :, low] = total.astype(BF16)
+
+        @pl.loop(0, NG)
+        def _(f):
+            gw = nn(ht[f], dval[:, :, low].reshape(2 * TOK, DH))
+            gbuf[f, :, :, low] = gw.astype(BF16).reshape(NY, ROWS, DH)
+
+        pair_x = functools.partial(rs1_x, g)
+        pair_y = functools.partial(rs1_y, g)
+        along("rs1", (pair_x, pair_x), (pair_y, pair_y))
+
     dx[c] = dval[c]
     go(remote(dval.at[o], dx.at[c], sib_s.at[5], sib_r.at[5], sibling), "dx")
-
-    @pl.loop(0, NG)
-    def _(g):
-        gw = nn(ht[g], dval[...].reshape(2 * TOK, HALF))
-        gbuf[g] = gw.astype(BF16).reshape(NY, ROWS, HALF)
-
-    def rs1_x(k):
-        return remote(
-            gbuf.at[pl.ds(x_peer(k) * ZH, ZH)], r1a.at[k - 1], rs1_s.at[k - 1], rs1_r.at[k - 1],
-            dev(x_peer(k), z, y),
-        )
-
-    def rs1_y(k):
-        return remote(
-            gbuf.at[:, y_peer(k)], r1b.at[k - 1], rs1_s.at[k - 1], rs1_r.at[k - 1], dev(x, z, y_peer(k))
-        )
 
     def rs2_y(k):
         return remote(
@@ -359,8 +370,6 @@
             s1b.at[pl.ds(x_peer(k) * ZH, ZH)], r2.at[k - 1], rs2_s.at[k - 1], rs2_r.at[k - 1],
             dev(x_peer(k), z, y),
         )
-
-    along("rs1", (rs1_x, rs1_x), (rs1_y, rs1_y))
 
     now("ag3")
     values = jnp.zeros((2 * TOK, HALF), F32)
@@ -369,29 +378,18 @@
     values = values.astype(BF16)
     vw[4] = values[:TOK]
     vw[5] = values[TOK:]
-    for k in (1, 2):
-        go(
-            remote(vw.at[4:6], vw.at[pl.ds((2 - k) * 2, 2)], v_s.at[k - 1], v_r.at[k - 1], chip(k) * 2 + c),
-            "none",
-        )
-        at = vw.at[pl.ds((2 - k) * 2, 2)]
-        later("v", lambda at=at, k=k: arrived(at, v_s.at[k - 1], v_r.at[k - 1]))
-    pending[:] = [p for p in pending if p[0] != "none"]
+    for g in range(2):
+        low = slice(g * DH, (g + 1) * DH)
+        for k in (1, 2):
+            i = g * 2 + k - 1
+            at = vw.at[pl.ds((2 - k) * 2, 2), :, low]
+            copy = remote(vw.at[4:6, :, low], at, v_s.at[i], v_r.at[i], chip(k) * 2 + c)
+            copy.start()
+            later("sent", copy.wait_send)
+            later("v%d" % g, lambda at=at, i=i: arrived(at, v_s.at[i], v_r.at[i]))
     go(remote(w2.at[c], w2.at[c], sib_s.at[4], sib_r.at[4], sibling), "none")
     pending[:] = [p for p in pending if p[0] != "none"]
     later("w2", lambda: arrived(w2.at[o], sib_s.at[4], sib_r.at[4]))
-
-    now("dx")
-    now("w2")
-
-    @pl.loop(0, NG)
-    def _(g):
-        both = nt(dx[0], w2[0, g].reshape(PG, HALF)) + nt(dx[1], w2[1, g].reshape(PG, HALF))
-        ghbuf[:, pl.ds(aligned(g * PG, PG), PG)] = nn(both.astype(BF16), perm[...]).astype(BF16)
-
-    copy = pltpu.make_async_copy(ghbuf, gh_out, loc.at[10])
-    copy.start()
-    later("sent", copy.wait)
 
     now("rs1")
 
@@ -432,26 +430,39 @@
         ring("rs3", rs3, rs3_in)
         r3[z] = z3[z]
 
+    now("dx")
+    now("w2")
+
+    @pl.loop(0, NG)
+    def _(g):
+        both = nt(dx[0], w2[0, g].reshape(PG, HALF)) + nt(dx[1], w2[1, g].reshape(PG, HALF))
+        ghbuf[:, pl.ds(aligned(g * PG, PG), PG)] = nn(both.astype(BF16), perm[...]).astype(BF16)
+
+    copy = pltpu.make_async_copy(ghbuf, gh_out, loc.at[10])
+    copy.start()
+    later("sent", copy.wait)
+
+    def stacked(ref, t, g):
+        return jnp.concatenate([ref[t, :, g * 512 + r * DH : g * 512 + (r + 1) * DH] for r in range(4)], 0)
+
     def path_b(t, g):
         keys = kw[pl.ds(t, 5), :, g * DH : (g + 1) * DH].reshape(5 * TOK, DH)
         vals = vw[pl.ds(t, 5), :, g * DH : (g + 1) * DH].reshape(5 * TOK, DH)
-        queries = []
+        grad = stacked(gobuf, t, g)
+        p = pbuf[t * 2 + g]
+        out = nn(p, vals).astype(BF16)
+        delta = jnp.sum(grad.astype(F32) * out.astype(F32), axis=1, keepdims=True)
+        dsbuf[...] = (p.astype(F32) * (nt(grad, vals) - delta)).astype(BF16)
+        dk = tn(dsbuf[...], stacked(qbuf, t, g)) * SCALE
+        dkw[pl.ds(t, 5), :, g * DH : (g + 1) * DH] += dk.reshape(5, TOK, DH)
+        dq = (nn(dsbuf[...], keys) * SCALE).astype(BF16)
         for r in range(4):
             qc = slice(g * 512 + r * DH, g * 512 + (r + 1) * DH)
-            p = pbuf[t * 2 + g, r * TOK : (r + 1) * TOK, :]
-            grad = gobuf[t, :, qc]
-            out = nn(p, vals).astype(BF16)
-            delta = jnp.sum(grad.astype(F32) * out.astype(F32), axis=1, keepdims=True)
-            ds = (p.astype(F32) * (nt(grad, vals) - delta)).astype(BF16)
-            obuf[t, :, qc] = out
-            dqbuf[t, :, qc] = (nn(ds, keys) * SCALE).astype(BF16)
-            dsbuf[r * TOK : (r + 1) * TOK, :] = ds
-            queries.append(qbuf[t, :, qc])
-        dk = tn(dsbuf[...], jnp.concatenate(queries, 0)) * SCALE
-        dkw[pl.ds(t, 5), :, g * DH : (g + 1) * DH] += dk.reshape(5, TOK, DH)
-
-    now("v")
+            obuf[t, :, qc] = out[r * TOK : (r + 1) * TOK]
+            dqbuf[t, :, qc] = dq[r * TOK : (r + 1) * TOK]
+
     for g in range(2):
+        now("v%d" % g)
         cols = slice(g * DH, (g + 1) * DH)
 
         @pl.loop(0, 2)
@@ -574,13 +585,13 @@
         DMA((11,)),
         DMA((9,)), DMA((9,)),
         DMA((5,)), DMA((6,)),
-        DMA((2,)), DMA((2,)),
+        DMA((4,)), DMA((4,)),
         DMA((4,)), DMA((4,)),
         DMA((10,)), DMA((10,)),
         DMA((NZ,)), DMA((NZ,)),
         DMA((NX - 1,)), DMA((NX - 1,)),
-        DMA((NX - 1,)), DMA((NX - 1,)),
-        DMA((NX - 1,)), DMA((NX - 1,)),
+        DMA((NY * (NX - 1),)), DMA((NY * (NX - 1),)),
+        DMA((2 * (NX - 1),)), DMA((2 * (NX - 1),)),
         DMA((NX - 1,)), DMA((NX - 1,)),
         DMA((NZ,)), DMA((NZ,)),
     ]

time: 76.5 us -> 70.5 us (0.922)
  Pallas kernels: 75.8 us -> 69.7 us
    pallas_call x1, Pallas kernels: 74.5 us -> 68.5 us  [shards(): pl.pallas_call(kernel, out_shape=shapes, in_specs=[hbm] * 7, out_specs=(a...]
where the time goes in v3:
time: 70.5 us; the launch traced here: 70.4 us
  Pallas kernels  69.7 us (99%)
    pallas_call x1, Pallas kernels, shards(): pl.pallas_call(kernel, out_shape=shapes, in_specs=[hbm] * 7, out_specs=(a...  68.5 us

profile of v3, /device:TPU:1, one launch (start us, length us, event | category | flops | bytes accessed | tf_op | source)
XLA Modules:
  0.0 70.4 jit_solution(10814034823164057501)
XLA Ops:
  0.6 68.5 %shard_map.126 = (bf16[128,2048]{1,0:T(8,128)(2,1)S(1)}, bf16[128,2048]{1,0:T(8,128)(2,1)S(1)}, bf16[128,512]{1,0:T(8,128)(2,1)S(1)}, bf16[128,2048]{1,0:T(8,128...) custom-call(bf16[128,2048]{1,0:T(8,128)(2,1)} %hid_ref.1, bf16[128,2048]{1,0:T(8,128)(2,1)} %q_ref.1, ...), custom_call_target="tpu_custom_call" | custom-call | tf_op jit(solution)/shard_map/pallas_call | solution.py:603
  69.1 1.3 %shard_map.127 = (bf16[128,2048]{1,0:T(8,128)(2,1)}, bf16[128,2048]{1,0:T(8,128)(2,1)}, bf16[128,512]{1,0:T(8,128)(2,1)}, bf16[128,2048]{1,0:T(8,128)(2,1)}, f32...) custom-call(bf16[128,2048]{1,0:T(8,128)(2,1)S(1)} %get-tuple-element.14.refs_0_, ...), custom_call_target="tpu_custom_call" | custom-call | tf_op jit(solution)/shard_map/pallas_call | solution.py:618

commit v4 on v3

--- a/solution.py
+++ b/solution.py
@@ -1,4 +1,3 @@
-import functools
 import math
 
 import jax
@@ -53,7 +52,7 @@
     o_out, dq_out, gk_out, gh_out, nw_out, nm_out, nv_out,
     hbuf, qbuf, gobuf, kw, vw, wsib, wz, w2, bias, perm, hp, ht, pbuf, dsbuf,
     dvw, dkw, dvs, dvr, dks, dkr, dksib, dksib_s, dval, dx,
-    gbuf, r1a, r1b, s1a, s1b, r2, t2, z3, r3, gx, obuf, dqbuf, adam, ghbuf,
+    gbuf, r1, s1, r2, t2, z3, r3, gx, obuf, dqbuf, adam, ghbuf,
     loc, sib_s, sib_r, k_s, k_r, v_s, v_r, dv_s, dv_r, dk_s, dk_r,
     ag1_s, ag1_r, ag2_s, ag2_r, ag3_s, ag3_r, rs1_s, rs1_r, rs2_s, rs2_r, rs3_s, rs3_r,
 ):
@@ -326,50 +325,42 @@
         hp[g] = nt(both, perm[...]).astype(BF16)
         ht[g] = nt(perm[...], both).astype(BF16)
 
-    def rs1_x(g, k):
-        low = slice(g * DH, (g + 1) * DH)
-        i = g * (NX - 1) + k - 1
-        return remote(
-            gbuf.at[pl.ds(x_peer(k) * ZH, ZH), :, :, low], r1a.at[k - 1, :, :, :, low], rs1_s.at[i], rs1_r.at[i],
-            dev(x_peer(k), z, y),
-        )
-
-    def rs1_y(g, k):
-        low = slice(g * DH, (g + 1) * DH)
-        i = g * (NX - 1) + k - 1
-        return remote(
-            gbuf.at[:, y_peer(k), :, low], r1b.at[k - 1, :, :, low], rs1_s.at[i], rs1_r.at[i],
-            dev(x, z, y_peer(k)),
-        )
-
+    def spot(k, j):
+        x_ = (x + jnp.where(c == 0, k, j)) % NX
+        y_ = (y + jnp.where(c == 0, j, k)) % NY
+        return x_, y_
+
+    def slab(k, j):
+        x_, y_ = spot(k, j)
+        return pl.ds(x_ * ZH, ZH), y_
+
+    def rs1(k, j):
+        x_, y_ = spot(k, 0)
+        i = j * (NX - 1) + k - 1
+        return remote(gbuf.at[slab(k, j)], r1.at[k - 1, j], rs1_s.at[i], rs1_r.at[i], dev(x_, z, y_))
+
+    def rs2(j):
+        x_, y_ = spot(0, j)
+        return remote(s1.at[j - 1], r2.at[j - 1], rs2_s.at[j - 1], rs2_r.at[j - 1], dev(x_, z, y_))
+
+    far = (2, 1, 3) if NX == 4 else tuple(range(1, NX))
     for g in range(2):
         now("dv%d" % g)
         low = slice(g * DH, (g + 1) * DH)
         total = dvw[4:6, :, low] + dvr[g * 2].astype(F32) + dvr[g * 2 + 1].astype(F32)
         dval[:, :, low] = total.astype(BF16)
 
-        @pl.loop(0, NG)
-        def _(f):
-            gw = nn(ht[f], dval[:, :, low].reshape(2 * TOK, DH))
-            gbuf[f, :, :, low] = gw.astype(BF16).reshape(NY, ROWS, DH)
-
-        pair_x = functools.partial(rs1_x, g)
-        pair_y = functools.partial(rs1_y, g)
-        along("rs1", (pair_x, pair_x), (pair_y, pair_y))
+    @pl.loop(0, NG)
+    def _(f):
+        gw = nn(ht[f], dval[...].reshape(2 * TOK, HALF))
+        gbuf[f] = gw.astype(BF16).reshape(NY, ROWS, HALF)
+
+    for j in far + (0,):
+        for k in far:
+            go(rs1(k, j), "rs1_%d" % j)
 
     dx[c] = dval[c]
     go(remote(dval.at[o], dx.at[c], sib_s.at[5], sib_r.at[5], sibling), "dx")
-
-    def rs2_y(k):
-        return remote(
-            s1a.at[:, y_peer(k)], r2.at[k - 1], rs2_s.at[k - 1], rs2_r.at[k - 1], dev(x, z, y_peer(k))
-        )
-
-    def rs2_x(k):
-        return remote(
-            s1b.at[pl.ds(x_peer(k) * ZH, ZH)], r2.at[k - 1], rs2_s.at[k - 1], rs2_r.at[k - 1],
-            dev(x_peer(k), z, y),
-        )
 
     now("ag3")
     values = jnp.zeros((2 * TOK, HALF), F32)
@@ -391,25 +382,28 @@
     pending[:] = [p for p in pending if p[0] != "none"]
     later("w2", lambda: arrived(w2.at[o], sib_s.at[4], sib_r.at[4]))
 
-    now("rs1")
-
-    def sum_zero():
-        part = gbuf[pl.ds(x * ZH, ZH)].astype(F32)
+    now("dx")
+    now("w2")
+
+    @pl.loop(0, NG)
+    def _(g):
+        both = nt(dx[0], w2[0, g].reshape(PG, HALF)) + nt(dx[1], w2[1, g].reshape(PG, HALF))
+        ghbuf[:, pl.ds(aligned(g * PG, PG), PG)] = nn(both.astype(BF16), perm[...]).astype(BF16)
+
+    copy = pltpu.make_async_copy(ghbuf, gh_out, loc.at[10])
+    copy.start()
+    later("sent", copy.wait)
+
+    for j in far + (0,):
+        now("rs1_%d" % j)
+        part = gbuf[slab(0, j)].astype(F32)
         for k in range(1, NX):
-            part = part + r1a[k - 1].astype(F32)
-        s1a[...] = part.astype(BF16)
-        t2[...] = s1a[:, y].astype(F32)
-
-    def sum_one():
-        part = gbuf[:, y].astype(F32)
-        for k in range(1, NY):
-            part = part + r1b[k - 1].astype(F32)
-        s1b[...] = part.astype(BF16)
-        t2[...] = s1b[pl.ds(x * ZH, ZH)].astype(F32)
-
-    on_core(0, sum_zero)
-    on_core(1, sum_one)
-    along("rs2", (rs2_y, rs2_y), (rs2_x, rs2_x))
+            part = part + r1[k - 1, j].astype(F32)
+        if j == 0:
+            t2[...] = part
+        else:
+            s1[j - 1] = part.astype(BF16)
+            go(rs2(j), "rs2")
 
     def rs3(k):
         z_ = (z + k) % NZ
@@ -429,18 +423,6 @@
             z3[zz] = jnp.concatenate([part[zz, :, :128], part[zz, :, 128:]], 0).astype(BF16)
         ring("rs3", rs3, rs3_in)
         r3[z] = z3[z]
-
-    now("dx")
-    now("w2")
-
-    @pl.loop(0, NG)
-    def _(g):
-        both = nt(dx[0], w2[0, g].reshape(PG, HALF)) + nt(dx[1], w2[1, g].reshape(PG, HALF))
-        ghbuf[:, pl.ds(aligned(g * PG, PG), PG)] = nn(both.astype(BF16), perm[...]).astype(BF16)
-
-    copy = pltpu.make_async_copy(ghbuf, gh_out, loc.at[10])
-    copy.start()
-    later("sent", copy.wait)
 
     def stacked(ref, t, g):
         return jnp.concatenate([ref[t, :, g * 512 + r * DH : g * 512 + (r + 1) * DH] for r in range(4)], 0)
@@ -569,10 +551,8 @@
         V((2, TOK, HALF), BF16),
         V((2, TOK, HALF), BF16),
         V((NG, NY, ROWS, HALF), BF16),
-        V((NX - 1, ZH, NY, ROWS, HALF), BF16),
-        V((NY - 1, NG, ROWS, HALF), BF16),
-        V((ZH, NY, ROWS, HALF), BF16),
-        V((NG, ROWS, HALF), BF16),
+        V((NX - 1, NY, ZH, ROWS, HALF), BF16),
+        V((NY - 1, ZH, ROWS, HALF), BF16),
         V((NX - 1, ZH, ROWS, HALF), BF16),
         V((ZH, ROWS, HALF), F32),
         V((NZ, 16, 128), BF16),
@@ -591,7 +571,7 @@
         DMA((NZ,)), DMA((NZ,)),
         DMA((NX - 1,)), DMA((NX - 1,)),
         DMA((NY * (NX - 1),)), DMA((NY * (NX - 1),)),
-        DMA((2 * (NX - 1),)), DMA((2 * (NX - 1),)),
+        DMA((NY * (NX - 1),)), DMA((NY * (NX - 1),)),
         DMA((NX - 1,)), DMA((NX - 1,)),
         DMA((NZ,)), DMA((NZ,)),
     ]

time: 70.5 us -> 68.2 us (0.967)
  Pallas kernels: 69.7 us -> 67.5 us
    pallas_call x1, Pallas kernels: 68.5 us -> 66.2 us  [shards(): pl.pallas_call(kernel, out_shape=shapes, in_specs=[hbm] * 7, out_specs=(a...]
where the time goes in v4:
time: 68.2 us; the launch traced here: 68.1 us
  Pallas kernels  67.5 us (99%)
    pallas_call x1, Pallas kernels, shards(): pl.pallas_call(kernel, out_shape=shapes, in_specs=[hbm] * 7, out_specs=(a...  66.2 us

profile of v4, /device:TPU:1, one launch (start us, length us, event | category | flops | bytes accessed | tf_op | source)
XLA Modules:
  0.0 68.1 jit_solution(9464441784950673338)
XLA Ops:
  0.6 66.2 %shard_map.126 = (bf16[128,2048]{1,0:T(8,128)(2,1)S(1)}, bf16[128,2048]{1,0:T(8,128)(2,1)S(1)}, bf16[128,512]{1,0:T(8,128)(2,1)S(1)}, bf16[128,2048]{1,0:T(8,128...) custom-call(bf16[128,2048]{1,0:T(8,128)(2,1)} %hid_ref.1, bf16[128,2048]{1,0:T(8,128)(2,1)} %q_ref.1, ...), custom_call_target="tpu_custom_call" | custom-call | tf_op jit(solution)/shard_map/pallas_call | solution.py:583
  66.9 1.3 %shard_map.127 = (bf16[128,2048]{1,0:T(8,128)(2,1)}, bf16[128,2048]{1,0:T(8,128)(2,1)}, bf16[128,512]{1,0:T(8,128)(2,1)}, bf16[128,2048]{1,0:T(8,128)(2,1)}, f32...) custom-call(bf16[128,2048]{1,0:T(8,128)(2,1)S(1)} %get-tuple-element.14.refs_0_, ...), custom_call_target="tpu_custom_call" | custom-call | tf_op jit(solution)/shard_map/pallas_call | solution.py:598

commit v5 on v4

--- a/solution.py
+++ b/solution.py
@@ -350,10 +350,10 @@
         total = dvw[4:6, :, low] + dvr[g * 2].astype(F32) + dvr[g * 2 + 1].astype(F32)
         dval[:, :, low] = total.astype(BF16)
 
-    @pl.loop(0, NG)
-    def _(f):
-        gw = nn(ht[f], dval[...].reshape(2 * TOK, HALF))
-        gbuf[f] = gw.astype(BF16).reshape(NY, ROWS, HALF)
+        @pl.loop(0, NG)
+        def _(f):
+            gw = nn(ht[f], dval[:, :, low].reshape(2 * TOK, DH))
+            gbuf[f, :, :, low] = gw.astype(BF16).reshape(NY, ROWS, DH)
 
     for j in far + (0,):
         for k in far:

time: 68.2 us -> 68.1 us (level)
  no operation moved by 1% of the time
where the time goes in v5:
time: 68.1 us; the launch traced here: 67.9 us
  Pallas kernels  67.3 us (99%)
    pallas_call x1, Pallas kernels, shards(): pl.pallas_call(kernel, out_shape=shapes, in_specs=[hbm] * 7, out_specs=(a...  66.1 us

profile of v5, /device:TPU:1, one launch (start us, length us, event | category | flops | bytes accessed | tf_op | source)
XLA Modules:
  0.0 67.9 jit_solution(5016123589007334946)
XLA Ops:
  0.6 66.1 %shard_map.126 = (bf16[128,2048]{1,0:T(8,128)(2,1)S(1)}, bf16[128,2048]{1,0:T(8,128)(2,1)S(1)}, bf16[128,512]{1,0:T(8,128)(2,1)S(1)}, bf16[128,2048]{1,0:T(8,128...) custom-call(bf16[128,2048]{1,0:T(8,128)(2,1)} %hid_ref.1, bf16[128,2048]{1,0:T(8,128)(2,1)} %q_ref.1, ...), custom_call_target="tpu_custom_call" | custom-call | tf_op jit(solution)/shard_map/pallas_call | solution.py:583
  66.7 1.3 %shard_map.127 = (bf16[128,2048]{1,0:T(8,128)(2,1)}, bf16[128,2048]{1,0:T(8,128)(2,1)}, bf16[128,512]{1,0:T(8,128)(2,1)}, bf16[128,2048]{1,0:T(8,128)(2,1)}, f32...) custom-call(bf16[128,2048]{1,0:T(8,128)(2,1)S(1)} %get-tuple-element.14.refs_0_, ...), custom_call_target="tpu_custom_call" | custom-call | tf_op jit(solution)/shard_map/pallas_call | solution.py:598
